TPU v7x, 32 devices: a whole 2x2x4 slice. The times are simulated.
32 devices in a mesh: tm: 16 (over z, y, core), region: 2 (over x).
Axes of the slice: x: 2, y: 2, z: 4, core: 2. Of those that a mesh axis runs over, the one named last changes fastest.
Arguments:
- waveform: bfloat16 [192, 131072], P('region', 'tm'), may hold values from -220 to 220
- station_order: int32 [192], P('region'), may hold values from 0 to 191, each once
- library: float32 [128, 24, 200], P('tm'), may hold values from -6 to 6
- owner: int32 [4], replicated, may hold values from 0 to 15
- channels: int32 [4, 8, 24], replicated, may hold values from 0 to 191, as said below
Outputs:
- detection: float32 [4, 8, 131072], P(None, 'region', 'tm')
Inputs may be any that keep to these rules, and one draw needn't show every extreme that they name: `channels`: within one template the 24 station channel ids differ.
All inputs are finite; a program needn't handle non-finite values.
Results may differ from a plain program's by a relative error of at most 0.003.
Values may be sent and summed in bfloat16 or wider, within the bound.
A program may use at most 64 MiB of HBM per device.

v0:
```python
import functools
import jax
import jax.numpy as jnp
from jax import lax
from jax.experimental import pallas as pl
from jax.experimental.pallas import tpu as pltpu
from jax.sharding import PartitionSpec as P

water_level = 4.0
eps = 1e-06
unroll = 16


def prepare_kernel(steps, count, owner_ref, library_ref, x_ref, inv_ref, out_ref, part, full, got, send_sems, recv_sems):
    me = lax.axis_index("tm")
    region = lax.axis_index("region")
    barrier = pltpu.get_barrier_semaphore()
    for d in range(1, count):
        peer = lax.rem(me + d, count)
        pl.semaphore_signal(barrier, inc=1, device_id=(peer, region), device_id_type=pl.DeviceIdType.MESH)

    panel = library_ref[...]
    taps = panel.shape[1]
    rows = panel.shape[0] // 16
    centred = panel - jnp.sum(panel, axis=1, keepdims=True) / taps
    normed = centred / jnp.sqrt(jnp.sum(centred * centred, axis=1, keepdims=True) + eps)
    mirror = lax.broadcasted_iota(jnp.int32, (taps, 256), 0) + lax.broadcasted_iota(jnp.int32, (taps, 256), 1)
    mirror = (mirror == 255).astype(jnp.float32).astype(jnp.bfloat16)
    turned = jnp.dot(normed.astype(jnp.bfloat16), mirror, preferred_element_type=jnp.float32)
    turned = turned.reshape(rows, 16, 256)
    if part.shape[0] > steps * rows:
        part[steps * rows :] = jnp.zeros((part.shape[0] - steps * rows, 16, 256), jnp.bfloat16)
    for s in range(steps):
        mine = jnp.where(owner_ref[s] == me, jnp.float32(1), jnp.float32(0))
        part[s * rows : (s + 1) * rows] = (turned * mine).astype(jnp.bfloat16)

    chans = x_ref.shape[0]
    blocks = x_ref.shape[1]
    group = 4
    chunks = chans // group
    offsets = lax.broadcasted_iota(jnp.int32, (384, 128), 0) - lax.broadcasted_iota(jnp.int32, (384, 128), 1)
    band = ((offsets >= 0) & (offsets < taps)).astype(jnp.float32).astype(jnp.bfloat16)

    def chunk(i, carry):
        x = x_ref[pl.ds(i * group, group)].reshape(group * blocks, 384).astype(jnp.float32)
        square = x * x
        high = square.astype(jnp.bfloat16)
        low = (square - high.astype(jnp.float32)).astype(jnp.bfloat16)
        energy = jnp.dot(high, band, preferred_element_type=jnp.float32)
        energy = energy + jnp.dot(low, band, preferred_element_type=jnp.float32)
        inv_ref[pl.ds(i * group, group)] = lax.rsqrt(energy + taps * water_level).reshape(group, blocks, 128)
        return carry

    phases = 2

    def scales(phase):
        lax.fori_loop(phase * chunks // phases, (phase + 1) * chunks // phases, chunk, 0)

    pl.semaphore_wait(barrier, count - 1)
    size = part.shape[0] // count
    own = pl.ds(me * size, size)

    def exchange(phase, source, target):
        copies = []
        for d in range(1, count):
            peer = lax.rem(me + d, count)
            copy = pltpu.make_async_remote_copy(
                src_ref=source(peer),
                dst_ref=target(d),
                send_sem=send_sems.at[phase, d - 1],
                recv_sem=recv_sems.at[phase, d - 1],
                device_id=(peer, region),
                device_id_type=pl.DeviceIdType.MESH,
            )
            copy.start()
            copies.append(copy)
        scales(phase)
        for copy in copies:
            copy.wait()

    exchange(0, lambda peer: part.at[pl.ds(peer * size, size)], lambda d: got.at[d - 1])
    total = part[own].astype(jnp.float32)
    for d in range(1, count):
        total = total + got[d - 1].astype(jnp.float32)
    full[own] = total.astype(jnp.bfloat16)
    exchange(1, lambda peer: full.at[own], lambda d: full.at[own])
    out_ref[...] = full[...].astype(jnp.float32)


def pair_kernel(code_ref, x_ref, inv_ref, taps_ref, out_ref, acc_ref, list_ref):
    templates = out_ref.shape[0]

    def compact(i, filled):
        code = code_ref[i]
        list_ref[filled] = code
        return filled + jnp.where(code >= 0, 1, 0)

    count = lax.fori_loop(0, code_ref.shape[0], compact, 0, unroll=8)
    for u in range(unroll):
        list_ref[count + u] = templates
    acc_ref[...] = jnp.zeros_like(acc_ref)
    lane = lax.broadcasted_iota(jnp.int32, (8, 128), 1)
    sub = lax.broadcasted_iota(jnp.int32, (8, 128), 0)

    def one_pair(code):
        template = code & 63
        col = (code >> 6) & 255
        row = code >> 14
        taps = taps_ref[pl.ds(row, 1), :]
        first = jnp.broadcast_to(taps[:, :128], (8, 128))
        second = jnp.broadcast_to(taps[:, 128:], (8, 128))
        first = pltpu.roll(first, 1, 1, stride=1, stride_axis=0)
        second = pltpu.roll(second, 1, 1, stride=1, stride_axis=0)
        zero = jnp.zeros((8, 128), jnp.float32)
        parts = [[], [], []]
        for a in range(16):
            one = pltpu.roll(first, 8 * a, 1) if a else first
            two = pltpu.roll(second, 8 * a, 1) if a else second
            below = lane <= sub + 8 * a
            parts[0].append(jnp.where(below, two, zero))
            parts[1].append(jnp.where(below, one, two))
            parts[2].append(jnp.where(below, zero, one))
        matrix = jnp.concatenate(parts[0] + parts[1] + parts[2], axis=0).astype(jnp.bfloat16)
        product = jnp.dot(x_ref[col], matrix, preferred_element_type=jnp.float32)
        return template, product * inv_ref[col]

    def group(i, carry):
        done = [one_pair(list_ref[i * unroll + u]) for u in range(unroll)]
        for template, value in done:
            acc_ref[template] += value
        return carry

    lax.fori_loop(0, (count + unroll - 1) // unroll, group, 0)
    out_ref[...] = acc_ref[:templates]


def finish_kernel(total_time, count, *refs):
    *parts, out_ref, sent, got, send_sems, recv_sems = refs
    me = lax.axis_index("tm")
    region = lax.axis_index("region")
    barrier = pltpu.get_barrier_semaphore()
    for d in range(1, count):
        peer = lax.rem(me + d, count)
        pl.semaphore_signal(barrier, inc=1, device_id=(peer, region), device_id_type=pl.DeviceIdType.MESH)
    held = out_ref.shape[0]
    stacked = parts[0][...]
    for other in parts[1:]:
        stacked = stacked + other[...]
    out_ref[...] = stacked
    power = jnp.sum(stacked * stacked, axis=1)
    power = jnp.broadcast_to(jnp.sum(power, axis=1, keepdims=True), (held, 128))
    sent[...] = power
    pl.semaphore_wait(barrier, count - 1)
    copies = []
    for d in range(1, count):
        peer = lax.rem(me + d, count)
        copy = pltpu.make_async_remote_copy(
            src_ref=sent,
            dst_ref=got.at[d - 1],
            send_sem=send_sems.at[d - 1],
            recv_sem=recv_sems.at[d - 1],
            device_id=(peer, region),
            device_id_type=pl.DeviceIdType.MESH,
        )
        copy.start()
        copies.append(copy)
    for copy in copies:
        copy.wait()
    power = power + jnp.sum(got[...], axis=0)
    factor = lax.rsqrt(power / total_time + eps)
    out_ref[...] = out_ref[...] * factor[:, None, :]


def pair_lists(station_order, channels, groups):
    steps, templates, used = channels.shape
    per_group = templates // groups
    length = steps * per_group * used
    grouped = channels.reshape(steps, groups, per_group, used).transpose(1, 0, 2, 3).reshape(groups, length)
    slot = jnp.arange(length, dtype=jnp.int32)
    step = slot // (per_group * used)
    inner = slot % (per_group * used)
    match = (grouped[:, :, None] == station_order[None, None, :]).astype(jnp.int32)
    local = jnp.sum(match, axis=2)
    col = jnp.sum(match * jnp.arange(station_order.shape[0], dtype=jnp.int32), axis=2)
    row = step * (templates * used) + jnp.arange(groups, dtype=jnp.int32)[:, None] * (per_group * used) + inner
    template = slot // used
    code = (row << 14) | (col << 6) | template
    return jnp.where(local > 0, code, -1)


def body(waveform, station_order, library, owner, channels):
    chan_local, time_local = waveform.shape
    num_blocks = time_local // 128
    steps, templates, used = channels.shape
    tap_count = library.shape[2]
    tm_size = lax.axis_size("tm")
    regions = lax.axis_size("region")
    per_group = templates // regions
    held = steps * per_group
    total_time = time_local * tm_size

    rim = lax.ppermute(waveform[:, :256], "tm", [(i, i - 1) for i in range(1, tm_size)])
    rim = jnp.where(jnp.arange(256)[None, :] < tap_count - 1, rim, jnp.zeros_like(rim))

    blocked = waveform.reshape(chan_local, num_blocks, 128)
    rim_blocks = rim.reshape(chan_local, 2, 128)
    extended = jnp.concatenate([blocked, rim_blocks], axis=1)
    windows = jnp.concatenate([extended[:, i : i + num_blocks] for i in range(3)], axis=2)

    vmem = pl.BlockSpec(memory_space=pltpu.VMEM)
    smem = pl.BlockSpec(memory_space=pltpu.SMEM)
    tap_rows = steps * templates * used
    tiles = -(-tap_rows // (16 * tm_size)) * tm_size
    tile = (tiles, 16, 256)
    inv_scale, taps = pl.pallas_call(
        functools.partial(prepare_kernel, steps, tm_size),
        out_shape=[
            jax.ShapeDtypeStruct((chan_local, num_blocks, 128), jnp.float32),
            jax.ShapeDtypeStruct(tile, jnp.float32),
        ],
        in_specs=[smem, vmem, vmem],
        out_specs=[vmem, vmem],
        scratch_shapes=[
            pltpu.VMEM(tile, jnp.bfloat16),
            pltpu.VMEM(tile, jnp.bfloat16),
            pltpu.VMEM((tm_size - 1, tiles // tm_size, 16, 256), jnp.bfloat16),
            pltpu.SemaphoreType.DMA((2, tm_size - 1)),
            pltpu.SemaphoreType.DMA((2, tm_size - 1)),
        ],
        compiler_params=pltpu.CompilerParams(
            collective_id=0, has_side_effects=True, vmem_limit_bytes=40 * 2**20
        ),
        name="prepare",
    )(owner, library.reshape(templates * used, tap_count), windows)
    taps = taps.reshape(tiles * 16, 256)

    codes = pair_lists(station_order, channels, regions)
    me = lax.axis_index("region")

    def partial_sums(group):
        return pl.pallas_call(
            pair_kernel,
            out_shape=jax.ShapeDtypeStruct((held, num_blocks, 128), jnp.float32),
            in_specs=[smem, vmem, vmem, vmem],
            out_specs=vmem,
            scratch_shapes=[
                pltpu.VMEM((held + 1, num_blocks, 128), jnp.float32),
                pltpu.SMEM((held * used + unroll,), jnp.int32),
            ],
            compiler_params=pltpu.CompilerParams(vmem_limit_bytes=40 * 2**20),
            cost_estimate=pl.CostEstimate(flops=held * used * 64 * 384 * 256, bytes_accessed=9 * 2**20, transcendentals=0),
            name="pairs",
        )(lax.dynamic_index_in_dim(codes, group, 0, False), windows, inv_scale, taps)

    arrived = []
    for shift in range(1, regions):
        part = partial_sums((me + shift) % regions)
        arrived.append(lax.ppermute(part, "region", [(i, (i + shift) % regions) for i in range(regions)]))
    arrived.append(partial_sums(me))
    result = pl.pallas_call(
        functools.partial(finish_kernel, total_time, tm_size),
        out_shape=jax.ShapeDtypeStruct((held, num_blocks, 128), jnp.float32),
        in_specs=[vmem] * len(arrived),
        out_specs=vmem,
        scratch_shapes=[
            pltpu.VMEM((held, 128), jnp.float32),
            pltpu.VMEM((tm_size - 1, held, 128), jnp.float32),
            pltpu.SemaphoreType.DMA((tm_size - 1,)),
            pltpu.SemaphoreType.DMA((tm_size - 1,)),
        ],
        compiler_params=pltpu.CompilerParams(
            collective_id=1, has_side_effects=True, vmem_limit_bytes=40 * 2**20
        ),
        name="finish",
    )(*arrived)
    return result.reshape(steps, per_group, time_local)


def solution(mesh):
    in_specs = (P("region", "tm"), P("region"), P("tm", None, None), P(), P())
    out_specs = P(None, "region", "tm")
    return jax.shard_map(body, mesh=mesh, in_specs=in_specs, out_specs=out_specs, check_vma=False)
```

profile of v0, /device:TPU:0, one launch (start us, length us, event | category | flops | bytes accessed | tf_op | source)
XLA Modules:
  0.0 69.3 jit_solution(15344108003445229747)
XLA Ops:
  0.0 0.8 %slice.9 = bf16[96,256]{1,0:T(8,128)(2,1)S(1)} slice(bf16[96,8192]{1,0:T(8,128)(2,1)} %param.5), slice={[0:96], [0:256]} | slice | bytes 98304 | tf_op jit(solution)/shard_map/slice | solution.py:202
  0.8 1.3 %collective-permute-start = (bf16[96,256]{1,0:T(8,128)(2,1)S(1)}, bf16[96,256]{1,0:T(8,128)(2,1)S(1)}, u32[]{:S(2)}, u32[]{:S(2)}) collective-permute-start(bf16[96,256]{1,0:T(8,128)(2,1)S(1)} %slice.9), channel_id=1, source_target_pairs={{2,0},{4,2},{6,4},{8,6},{10,8},{12,10},{14,12},{16,14},{18,16},{20... | collective-permute-start | bytes 147464 | tf_op jit(solution)/shard_map/ppermute | solution.py:202
  2.1 0.7 %copy.10 = s32[4,2,4,24]{3,2,0,1:T(4,128)S(1)} copy(s32[4,2,4,24]{3,2,1,0:T(4,128)} %bitcast.15) | data formatting | bytes 6144 | tf_op jit(solution)/shard_map/reshape | solution.py:178
  2.9 0.1 eq.19
  3.0 1.8 %copy.8 = bf16[12,8,64,128]{3,2,1,0:T(8,128)(2,1)S(1)} copy(bf16[12,8,64,128]{3,1,2,0:T(8,128)(2,1)} %bitcast.13) | data formatting | bytes 3145728
  4.8 0.0 copy-start.2
  4.8 0.1 constant_dynamic-update-slice_fusion.1
  4.9 0.5 copy-done.2
  5.5 0.1 fusion.1
  5.6 0.1 compare_select_fusion.1
  5.7 0.0 collective-permute-done
  5.8 0.1 constant_dynamic-update-slice_fusion
  5.8 1.0 %fusion.11 = (bf16[96,64,128]{2,1,0:T(8,128)(2,1)S(1)}, bf16[96,64,128]{2,1,0:T(8,128)(2,1)S(1)}) fusion(bf16[96,66,128]{2,1,0:T(8,128)(2,1)S(1)} %constant_dynamic-update-slice_fusion), kind=kLoop, calls=%fused_computation.30 | loop fusion | bytes 6291456 | tf_op jit(solution)/shard_map/slice | solution.py:208
  6.8 0.0 copy-start
  6.8 0.0 copy-start.1
  6.8 0.8 %pad_maximum_fusion.x_ref = bf16[96,64,384]{2,1,0:T(8,128)(2,1)S(1)} fusion(bf16[96,64,128]{2,1,0:T(8,128)(2,1)S(1)} %get-tuple-element.14, bf16[96,64,128]{2,1,0:T(8,128)(2,1)S(1)} %get-tuple-element.13, bf16[96,64,128]{2,1,0:T(8,128)(2,1)S(1)} %bitcast.12), kind=kLoop, calls=%fused_computation | loop fusion | flops 14155776 | bytes 9437184 | tf_op jit(solution)/shard_map/concatenate | solution.py:208
  7.6 0.1 copy-done
  7.7 23.1 %prepare.1 = (f32[96,64,128]{2,1,0:T(8,128)S(1)}, f32[48,16,256]{2,1,0:T(8,128)S(1)}) custom-call(s32[4]{0:T(128)S(1)} %copy-done.1, f32[192,200]{1,0:T(8,128)S(1)} %bitcast.10, bf16[96,64,384]{2,1,0:T(8,128)(2,1)S(1)} %pad_maximum_fusion.x_ref), custom_call_target="tpu_custom_call" | custom-call | tf_op jit(solution)/shard_map/prepare/pallas_call | solution.py:215
  30.9 12.3 %pairs.2 = f32[16,64,128]{2,1,0:T(8,128)S(1)} custom-call(s32[384]{0:T(512)S(1)} %get-tuple-element.12.code_ref, bf16[96,64,384]{2,1,0:T(8,128)(2,1)S(1)} %pad_maximum_fusion.x_ref, f32[96,64,128]{2,1,0:T(8,128)S(1)} %get-tuple-element.7.inv_ref, f32[768,256]{1,0:T(8,128)S(1)} %bitcast.8), custom_call_target="tpu_custom_call" | custom-call | flops 2415919104 | bytes 9437184 | tf_op jit(solution)/shard_map/pairs/pallas_call | solution.py:241
  43.2 0.7 %collective-permute-start.1 = (f32[16,64,128]{2,1,0:T(8,128)S(1)}, f32[16,64,128]{2,1,0:T(8,128)S(1)}, u32[]{:S(2)}, u32[]{:S(2)}) collective-permute-start(f32[16,64,128]{2,1,0:T(8,128)S(1)} %pairs.2), channel_id=1, source_target_pairs={{0,1},{1,0},{2,3},{3,2},{4,5},{5,4},{6,7},{7,6},{8,9},{9,8},{10,11... | collective-permute-start | bytes 1572872 | tf_op jit(solution)/shard_map/ppermute | solution.py:258
  43.9 12.3 %pairs.3.refs_1_ = f32[16,64,128]{2,1,0:T(8,128)S(1)} custom-call(s32[384]{0:T(512)S(1)} %get-tuple-element.11.code_ref, bf16[96,64,384]{2,1,0:T(8,128)(2,1)S(1)} %pad_maximum_fusion.x_ref, f32[96,64,128]{2,1,0:T(8,128)S(1)} %get-tuple-element.7.inv_ref, f32[768,256]{1,0:T(8,128)S(1)} %bitcast.9), custom_call_target="tpu_custom_call" | custom-call | flops 2415919104 | bytes 9437184 | tf_op jit(solution)/shard_map/pairs/pallas_call | solution.py:241
  56.3 1.7 %collective-permute-done.1.refs_0_ = f32[16,64,128]{2,1,0:T(8,128)S(1)} collective-permute-done((f32[16,64,128]{2,1,0:T(8,128)S(1)}, f32[16,64,128]{2,1,0:T(8,128)S(1)}, u32[]{:S(2)}, u32[]{:S(2)}) %collective-permute-start.1) | collective-permute-done | bytes 524320 | tf_op jit(solution)/shard_map/ppermute | solution.py:258
  58.0 10.3 %finish.1 = f32[16,64,128]{2,1,0:T(8,128)S(1)} custom-call(f32[16,64,128]{2,1,0:T(8,128)S(1)} %collective-permute-done.1.refs_0_, f32[16,64,128]{2,1,0:T(8,128)S(1)} %pairs.3.refs_1_), custom_call_target="tpu_custom_call" | custom-call | tf_op jit(solution)/shard_map/finish/pallas_call | solution.py:260
  68.3 1.0 %reshape.66 = f32[4,4,8192]{2,1,0:T(4,128)} reshape(f32[16,64,128]{2,1,0:T(8,128)S(1)} %finish.1) | data formatting | bytes 1048576 | tf_op jit(solution)/shard_map/reshape | solution.py:276
  (8 shorter events, 0.1 us)
Async XLA Ops:
  0.8 4.9 %collective-permute-start = (bf16[96,256]{1,0:T(8,128)(2,1)S(1)}, bf16[96,256]{1,0:T(8,128)(2,1)S(1)}, u32[]{:S(2)}, u32[]{:S(2)}) collective-permute-start(bf16[96,256]{1,0:T(8,128)(2,1)S(1)} %slice.9), channel_id=1, source_target_pairs={{2,0},{4,2},{6,4},{8,6},{10,8},{12,10},{14,12},{16,14},{18,16},{20... | collective-permute-start | bytes 147464 | tf_op jit(solution)/shard_map/ppermute | solution.py:202
  4.8 0.7 copy-start.2
  6.8 0.9 %copy-start = (f32[8,24,200]{2,1,0:T(8,128)S(1)}, f32[8,24,200]{2,1,0:T(8,128)}, u32[]{:S(2)}) copy-start(f32[8,24,200]{2,1,0:T(8,128)} %param.7) | copy-start | bytes 460804
  6.8 0.9 %copy-start.1 = (s32[4]{0:T(128)S(1)}, s32[4]{0:T(128)}, u32[]{:S(2)}) copy-start(s32[4]{0:T(128)} %owner_ref.1) | copy-start | bytes 52
  43.2 14.8 %collective-permute-start.1 = (f32[16,64,128]{2,1,0:T(8,128)S(1)}, f32[16,64,128]{2,1,0:T(8,128)S(1)}, u32[]{:S(2)}, u32[]{:S(2)}) collective-permute-start(f32[16,64,128]{2,1,0:T(8,128)S(1)} %pairs.2), channel_id=1, source_target_pairs={{0,1},{1,0},{2,3},{3,2},{4,5},{5,4},{6,7},{7,6},{8,9},{9,8},{10,11... | collective-permute-start | bytes 1572872 | tf_op jit(solution)/shard_map/ppermute | solution.py:258
where the time goes:
time: 69.5 us; the launch traced here: 69.3 us
  Pallas kernels  58.1 us (84%)
  local copies, waits for them, and re-layouts  6.34 us (9%)
  starting transfers between devices  2.01 us (3%)
  waiting for transfers between devices  1.72 us (2%)
  other arithmetic  1.01 us (1%)
    pallas_call x2, Pallas kernels, partial_sums(): pl.pallas_call(pair_kernel, out_shape=jax.ShapeDtypeStruct((held, num_blo...  24.6 us
    pallas_call x1, Pallas kernels, body(): pl.pallas_call(functools.partial(prepare_kernel, steps, tm_size), out_sha...  23.1 us
    pallas_call x1, Pallas kernels, body(): pl.pallas_call(functools.partial(finish_kernel, total_time, tm_size), out...  10.3 us
    unnamed x8, local copies, waits for them, and re-layouts  2.63 us
    ppermute x1, waiting for transfers between devices, body(): lax.ppermute(part, 'region', [(i, (i + shift) % regions) for i in range(r...  1.72 us
  transfers between devices with their start and end apart: 2, of which 1 were waited for; matrix products, arithmetic and copies ran while one was open for 4% of the time, Pallas kernels for 18%

commit v1 on v0

v1 whole, which is shorter than its diff:
```python
import functools
import jax
import jax.numpy as jnp
from jax import lax
from jax.experimental import pallas as pl
from jax.experimental.pallas import tpu as pltpu
from jax.sharding import PartitionSpec as P

water_level = 4.0
eps = 1e-06
offs = 32
depth = 256
rows_z = 288
unroll = 32
MESH = pl.DeviceIdType.MESH


def prepare_kernel(
    steps, count, owner_ref, library_ref, x_ref, edge_ref, z_ref, inv_ref, taps_ref,
    mine, got, sel, full, halo, halo_f, ext, halo_sems, one_send, one_recv, two_send, two_recv,
):
    me = lax.axis_index("tm")
    region = lax.axis_index("region")
    barrier = pltpu.get_barrier_semaphore()
    for d in range(1, count):
        pl.semaphore_signal(barrier, inc=1, device_id=(lax.rem(me + d, count), region), device_id_type=MESH)

    taps = library_ref.shape[1]
    tiles = mine.shape[0]
    panel = library_ref[...]
    centred = panel - jnp.sum(panel, axis=1, keepdims=True) / taps
    normed = centred / jnp.sqrt(jnp.sum(centred * centred, axis=1, keepdims=True) + eps)
    normed = jnp.concatenate([normed, jnp.zeros((panel.shape[0], depth - taps), jnp.float32)], axis=1)
    mine[...] = normed.astype(jnp.bfloat16).reshape(tiles, 16, depth)

    holders = [u * count // tiles for u in range(tiles)]
    my_tile = (me * tiles + count - 1) // count
    holding = my_tile * count // tiles == me
    my_tile = jnp.minimum(my_tile, tiles - 1)

    pl.semaphore_wait(barrier, count - 1)
    left = lax.rem(me + count - 1, count)
    edge_copy = pltpu.make_async_remote_copy(
        src_ref=edge_ref, dst_ref=halo, send_sem=halo_sems.at[0], recv_sem=halo_sems.at[1],
        device_id=(left, region), device_id_type=MESH,
    )
    edge_copy.start()

    def piece(u):
        return pltpu.make_async_remote_copy(
            src_ref=mine.at[u], dst_ref=got.at[me], send_sem=one_send.at[u], recv_sem=one_recv.at[me],
            device_id=(holders[u], region), device_id_type=MESH,
        )

    for u in range(tiles):
        @pl.when(me != holders[u])
        def _():
            piece(u).start()

    chans, blocks, _ = x_ref.shape
    lane = lax.broadcasted_iota(jnp.int32, (1, 128), 1)
    low_half = lane < 64
    spread = lax.broadcasted_iota(jnp.int32, (offs, depth), 1) - lax.broadcasted_iota(jnp.int32, (offs, depth), 0)
    band = ((spread >= 0) & (spread < taps)).astype(jnp.float32).astype(jnp.bfloat16)
    width = ext.shape[0]

    def channel(c, slot):
        ext[slot, 0:blocks] = x_ref[c].astype(jnp.float32)
        rim = halo_f[pl.ds(c, 1), :]
        ext[slot, blocks : blocks + 1] = rim[:, 0:128]
        ext[slot, blocks + 1 : blocks + 2] = rim[:, 128:256]
        x = [ext[slot, m : m + blocks] for m in range(3)]
        y = [pltpu.roll(v, 64, 1) for v in x]
        columns = []
        for m in range(3):
            second = jnp.where(low_half, y[m], y[m + 1]) if m < 2 else y[m]
            columns.append(jnp.concatenate([x[m], second], axis=0).T)
        z = jnp.concatenate([columns[0], columns[1], columns[2][: rows_z - 256]], axis=0)
        z_ref[c] = z.astype(jnp.bfloat16)
        square = z * z
        high = square.astype(jnp.bfloat16)
        low = (square - high.astype(jnp.float32)).astype(jnp.bfloat16)

        def both(v):
            return jnp.concatenate([v[0:depth], v[offs : offs + depth]], axis=1)

        energy = jnp.dot(band, both(high), preferred_element_type=jnp.float32)
        energy = energy + jnp.dot(band, both(low), preferred_element_type=jnp.float32)
        inv_ref[c] = lax.rsqrt(energy + taps * water_level)

    def windows(first, last):
        def group(i, carry):
            for slot in range(width):
                channel(i * width + slot, slot)
            return carry

        lax.fori_loop(first // width, last // width, group, 0)

    edge_copy.wait()
    inside = (me < count - 1) & (lax.broadcasted_iota(jnp.int32, (chans, depth), 1) < taps - 1)
    halo_f[...] = jnp.where(inside, halo[...].astype(jnp.float32), 0.0)
    split = chans // 3 // width * width
    windows(0, split)

    for u in range(tiles):
        @pl.when(me != holders[u])
        def _():
            piece(u).wait_send()

    def spread_copy(d):
        return pltpu.make_async_remote_copy(
            src_ref=sel, dst_ref=full.at[my_tile], send_sem=two_send.at[d - 1], recv_sem=two_recv.at[my_tile],
            device_id=(lax.rem(me + d, count), region), device_id_type=MESH,
        )

    @pl.when(holding)
    def _():
        for i in range(count):
            @pl.when(me != i)
            def _():
                pltpu.make_async_remote_copy(
                    src_ref=mine.at[0], dst_ref=got.at[i], send_sem=one_send.at[0], recv_sem=one_recv.at[i],
                    device_id=(left, region), device_id_type=MESH,
                ).wait_recv()
        got[me] = mine[my_tile]
        for s in range(steps):
            sel[s] = got[owner_ref[s]]
        full[my_tile] = sel[...]
        for d in range(1, count):
            spread_copy(d).start()

    windows(split, chans)

    for u in range(tiles):
        @pl.when(me != holders[u])
        def _():
            pltpu.make_async_remote_copy(
                src_ref=sel, dst_ref=full.at[u], send_sem=two_send.at[0], recv_sem=two_recv.at[u],
                device_id=(left, region), device_id_type=MESH,
            ).wait_recv()

    taps_ref[0 : tiles * steps * 16] = full[...].astype(jnp.float32).reshape(tiles * steps * 16, depth)
    taps_ref[tiles * steps * 16 :] = jnp.zeros((8, depth), jnp.float32)

    @pl.when(holding)
    def _():
        for d in range(1, count):
            spread_copy(d).wait_send()


def pair_kernel(code_ref, z_ref, inv_ref, taps_ref, out_ref, acc_ref, list_ref):
    templates = out_ref.shape[0]

    def compact(i, filled):
        code = code_ref[i]
        list_ref[filled] = code
        return filled + jnp.where(code >= 0, 1, 0)

    count = lax.fori_loop(0, code_ref.shape[0], compact, 0, unroll=8)
    for u in range(unroll):
        list_ref[count + u] = templates
    acc_ref[...] = jnp.zeros_like(acc_ref)

    def one_pair(code):
        template = code & 63
        col = (code >> 6) & 255
        row = code >> 14
        base = jnp.broadcast_to(taps_ref[pl.ds(row, 1)], (8, depth))
        base = pltpu.roll(base, 0, 1, stride=1, stride_axis=0)
        shifted = [base] + [pltpu.roll(base, a, 1) for a in range(8, offs, 8)]
        matrix = jnp.concatenate(shifted, axis=0).astype(jnp.bfloat16)
        window = jnp.concatenate([z_ref[col, 0:depth], z_ref[col, offs : offs + depth]], axis=1)
        product = jnp.dot(matrix, window, preferred_element_type=jnp.float32)
        return template, product * inv_ref[col]

    def group(i, carry):
        done = [one_pair(list_ref[i * unroll + u]) for u in range(unroll)]
        for template, value in done:
            acc_ref[template] += value
        return carry

    lax.fori_loop(0, (count + unroll - 1) // unroll, group, 0)
    out_ref[...] = acc_ref[:templates]


def finish_kernel(total_time, steps, count, regions, parts_ref, out_ref, sent, arrived, stacked, power_sent, power_got, x_send, x_recv, p_send, p_recv):
    me = lax.axis_index("tm")
    region = lax.axis_index("region")
    barrier = pltpu.get_barrier_semaphore()
    for d in range(1, regions):
        pl.semaphore_signal(barrier, inc=1, device_id=(me, lax.rem(region + d, regions)), device_id_type=MESH)
    for d in range(1, count):
        pl.semaphore_signal(barrier, inc=1, device_id=(lax.rem(me + d, count), region), device_id_type=MESH)
    held = out_ref.shape[0]
    per = held // steps

    def chunk(d, s):
        return pltpu.make_async_remote_copy(
            src_ref=sent.at[d - 1, s], dst_ref=arrived.at[d - 1, s], send_sem=x_send.at[d - 1, s], recv_sem=x_recv.at[d - 1, s],
            device_id=(me, lax.rem(region + d, regions)), device_id_type=MESH,
        )

    for s in range(steps):
        for d in range(1, regions):
            other = lax.rem(region + d, regions)
            sent[d - 1, s] = parts_ref[pl.ds(other * held + s * per, per)].astype(jnp.bfloat16)
        if s == 0:
            pl.semaphore_wait(barrier, count - 1 + regions - 1)
        for d in range(1, regions):
            chunk(d, s).start()
    lane = lax.broadcasted_iota(jnp.int32, (1, 128), 1)
    power = jnp.zeros((1, 128), jnp.float32)
    for s in range(steps):
        for d in range(1, regions):
            chunk(d, s).wait_recv()
        for k in range(per):
            at = s * per + k
            value = parts_ref[region * held + at]
            for d in range(1, regions):
                value = value + arrived[d - 1, s, k].astype(jnp.float32)
            total = jnp.sum(jnp.sum(value * value, axis=0, keepdims=True), axis=1, keepdims=True)
            power = power + jnp.where(lane == at, total, 0.0)
            upright = jnp.concatenate([value[:, :128], value[:, 128:]], axis=0).T
            stacked[at] = jnp.concatenate([upright[:64], upright[64:]], axis=1)
    power_sent[...] = power
    copies = []
    for d in range(1, count):
        copy = pltpu.make_async_remote_copy(
            src_ref=power_sent, dst_ref=power_got.at[d - 1], send_sem=p_send.at[d - 1], recv_sem=p_recv.at[d - 1],
            device_id=(lax.rem(me + d, count), region), device_id_type=MESH,
        )
        copy.start()
        copies.append(copy)
    for copy in copies:
        copy.wait_recv()
    power = power + jnp.sum(power_got[...], axis=0)
    factor = lax.rsqrt(power / total_time + eps)
    for at in range(held):
        one = jnp.sum(jnp.where(lane == at, factor, 0.0), axis=1, keepdims=True)
        out_ref[at] = stacked[at] * one
    for s in range(steps):
        for d in range(1, regions):
            chunk(d, s).wait_send()
    for copy in copies:
        copy.wait_send()


def pair_list(station_order, channels, regions):
    steps, templates, used = channels.shape
    per = templates // regions
    match = (channels.reshape(-1)[:, None] == station_order[None, :]).astype(jnp.int32)
    local = jnp.sum(match, axis=1)
    col = jnp.sum(match * jnp.arange(station_order.shape[0], dtype=jnp.int32)[None, :], axis=1)
    pair = jnp.arange(steps * templates * used, dtype=jnp.int32)
    step = pair // (templates * used)
    inner = pair % (templates * used)
    row = (inner // 16 * steps + step) * 16 + inner % 16
    k = inner // used
    template = (k // per) * (steps * per) + step * per + k % per
    code = (row << 14) | (col << 6) | template
    return jnp.where(local > 0, code, -1)


def body(waveform, station_order, library, owner, channels):
    chans, time_local = waveform.shape
    blocks = time_local // 128
    steps, templates, used = channels.shape
    tap_count = library.shape[2]
    count = lax.axis_size("tm")
    regions = lax.axis_size("region")
    per = templates // regions
    held = steps * per
    all_templates = steps * templates
    pairs = all_templates * used
    tiles = templates * used // 16
    lanes = time_local // offs
    wide = 4

    vmem = pl.BlockSpec(memory_space=pltpu.VMEM)
    smem = pl.BlockSpec(memory_space=pltpu.SMEM)
    dma = pltpu.SemaphoreType.DMA
    z, inv_scale, taps = pl.pallas_call(
        functools.partial(prepare_kernel, steps, count),
        out_shape=[
            jax.ShapeDtypeStruct((chans, rows_z, 128), jnp.bfloat16),
            jax.ShapeDtypeStruct((chans, offs, lanes), jnp.float32),
            jax.ShapeDtypeStruct((pairs + 8, depth), jnp.float32),
        ],
        in_specs=[smem, vmem, vmem, vmem],
        out_specs=[vmem, vmem, vmem],
        scratch_shapes=[
            pltpu.VMEM((tiles, 16, depth), jnp.bfloat16),
            pltpu.VMEM((count, 16, depth), jnp.bfloat16),
            pltpu.VMEM((steps, 16, depth), jnp.bfloat16),
            pltpu.VMEM((tiles, steps, 16, depth), jnp.bfloat16),
            pltpu.VMEM((chans, depth), jnp.bfloat16),
            pltpu.VMEM((chans, depth), jnp.float32),
            pltpu.VMEM((wide, blocks + 8, 128), jnp.float32),
            dma((2,)),
            dma((tiles,)),
            dma((count,)),
            dma((count - 1,)),
            dma((tiles,)),
        ],
        compiler_params=pltpu.CompilerParams(collective_id=0, has_side_effects=True, vmem_limit_bytes=40 * 2**20),
        name="prepare",
    )(owner, library.reshape(templates * used, tap_count), waveform.reshape(chans, blocks, 128), waveform[:, :depth])

    codes = pair_list(station_order, channels, regions)
    parts = pl.pallas_call(
        pair_kernel,
        out_shape=jax.ShapeDtypeStruct((all_templates, offs, lanes), jnp.float32),
        in_specs=[smem, vmem, vmem, vmem],
        out_specs=vmem,
        scratch_shapes=[
            pltpu.VMEM((all_templates + 1, offs, lanes), jnp.float32),
            pltpu.SMEM((pairs + unroll,), jnp.int32),
        ],
        compiler_params=pltpu.CompilerParams(vmem_limit_bytes=40 * 2**20),
        name="pairs",
    )(codes, z, inv_scale, taps)

    result = pl.pallas_call(
        functools.partial(finish_kernel, time_local * count, steps, count, regions),
        out_shape=jax.ShapeDtypeStruct((held, blocks, 128), jnp.float32),
        in_specs=[vmem],
        out_specs=vmem,
        scratch_shapes=[
            pltpu.VMEM((regions - 1, steps, per, offs, lanes), jnp.bfloat16),
            pltpu.VMEM((regions - 1, steps, per, offs, lanes), jnp.bfloat16),
            pltpu.VMEM((held, blocks, 128), jnp.float32),
            pltpu.VMEM((1, 128), jnp.float32),
            pltpu.VMEM((count - 1, 1, 128), jnp.float32),
            dma((regions - 1, steps)),
            dma((regions - 1, steps)),
            dma((count - 1,)),
            dma((count - 1,)),
        ],
        compiler_params=pltpu.CompilerParams(collective_id=1, has_side_effects=True, vmem_limit_bytes=40 * 2**20),
        name="finish",
    )(parts)
    return result.reshape(steps, per, time_local)


def solution(mesh):
    in_specs = (P("region", "tm"), P("region"), P("tm", None, None), P(), P())
    out_specs = P(None, "region", "tm")
    return jax.shard_map(body, mesh=mesh, in_specs=in_specs, out_specs=out_specs, check_vma=False)
```

time: 69.5 us -> 66.8 us (0.961)
  local copies, waits for them, and re-layouts: 6.34 us -> 11.7 us
  Pallas kernels: 58.1 us -> 54.5 us
  starting transfers between devices: 2.01 us -> 0 us
  waiting for transfers between devices: 1.72 us -> 0 us
  other arithmetic: 1.01 us -> 0.16 us
    unnamed x8 -> x17, local copies, waits for them, and re-layouts: 2.63 us -> 9.79 us
    pallas_call x4 -> x3, Pallas kernels: 58.1 us -> 54.5 us  [the longest x1 22.1 us: body(): pl.pallas_call(functools.partial(prepare_kernel, steps, count), out_shape...]
    ppermute x2 -> x0, starting transfers between devices: 2.01 us -> none  [the longest x1 1.28 us: body(): lax.ppermute(waveform[:, :256], 'tm', [(i, i - 1) for i in range(1, tm_si...]
    ppermute x2 -> x0, waiting for transfers between devices: 1.72 us -> none  [the longest x1 1.72 us: body(): lax.ppermute(part, 'region', [(i, (i + shift) % regions) for i in range(r...]
    slice x2 -> x1, local copies, waits for them, and re-layouts: 1.77 us -> 0.81 us  [body(): waveform[:, :depth]]
    concatenate x1 -> x0, other arithmetic: 0.76 us -> none  [body(): jnp.concatenate([extended[:, i:i + num_blocks] for i in range(3)], axis=2)]
    reshape x3 -> x1, local copies, waits for them, and re-layouts: 1.75 us -> 1.01 us  [body(): return result.reshape(steps, per, time_local)]
  transfers between devices with their start and end apart: 2 -> 0, of which waited for: 1 -> 0; matrix products, arithmetic and copies ran while one was open for 4% -> 0% of each run, Pallas kernels for 18% -> 0%
where the time goes in v1:
time: 66.8 us; the launch traced here: 66.5 us
  Pallas kernels  54.5 us (82%)
  local copies, waits for them, and re-layouts  11.7 us (18%)
    pallas_call x1, Pallas kernels, body(): pl.pallas_call(functools.partial(prepare_kernel, steps, count), out_shape...  22.1 us
    pallas_call x1, Pallas kernels, body(): pl.pallas_call(functools.partial(finish_kernel, time_local * count, steps...  18 us
    pallas_call x1, Pallas kernels, body(): pl.pallas_call(pair_kernel, out_shape=jax.ShapeDtypeStruct((all_templates...  14.4 us
    unnamed x17, local copies, waits for them, and re-layouts  9.79 us

profile of v1, /device:TPU:0, one launch (start us, length us, event | category | flops | bytes accessed | tf_op | source)
XLA Modules:
  0.0 66.5 jit_solution(16986194892524866368)
XLA Ops:
  0.0 0.0 copy-start.4
  0.0 0.0 copy-start.5
  0.0 0.0 copy-start.6
  0.0 0.0 copy-start.7
  0.0 1.9 %copy.6 = bf16[12,8,64,128]{3,2,1,0:T(8,128)(2,1)S(1)} copy(bf16[12,8,64,128]{3,1,2,0:T(8,128)(2,1)} %bitcast.5) | data formatting | bytes 3145728
  1.9 0.8 %slice.3.edge_ref = bf16[96,256]{1,0:T(8,128)(2,1)S(1)} slice(bf16[96,8192]{1,0:T(8,128)(2,1)} %param.5), slice={[0:96], [0:256]} | slice | bytes 98304 | tf_op jit(solution)/shard_map/slice | solution.py:307
  2.7 0.0 copy-done.4
  2.7 0.0 copy-done.5
  2.7 22.1 %prepare.1 = (bf16[96,288,128]{2,1,0:T(8,128)(2,1)S(1)}, f32[96,32,256]{2,1,0:T(8,128)S(1)}, f32[776,256]{1,0:T(8,128)S(1)}) custom-call(s32[4]{0:T(128)S(1)} %copy-done.5, f32[192,200]{1,0:T(8,128)S(1)} %bitcast.4, bf16[96,64,128]{2,1,0:T(8,128)(2,1)S(1)} %bitcast.3, bf16[96,256]{1,0:T(8,128)(2,1)S(1)} %slice.3.edge_ref), custom_call_target="tpu_custom_call" | custom-call | tf_op jit(solution)/shard_map/prepare/pallas_call | solution.py:282
  24.8 0.0 copy-start
  24.8 2.9 %copy-done = bf16[96,288,128]{2,1,0:T(8,128)(2,1)} copy-done((bf16[96,288,128]{2,1,0:T(8,128)(2,1)}, bf16[96,288,128]{2,1,0:T(8,128)(2,1)S(1)}, u32[]{:S(2)}) %copy-start) | copy-done | bytes 7077912
  27.7 0.0 copy-start.2
  27.7 0.9 %copy-done.2 = f32[776,256]{1,0:T(8,128)} copy-done((f32[776,256]{1,0:T(8,128)}, f32[776,256]{1,0:T(8,128)S(1)}, u32[]{:S(2)}) %copy-start.2) | copy-done | bytes 794648
  28.6 0.0 copy-done.6
  28.6 0.1 eq.19
  28.7 0.0 copy-done.7
  28.7 0.1 fusion
  28.9 0.0 copy-start.1
  28.9 3.0 %copy-done.1 = bf16[96,288,128]{2,1,0:T(8,128)(2,1)S(1)} copy-done((bf16[96,288,128]{2,1,0:T(8,128)(2,1)S(1)}, bf16[96,288,128]{2,1,0:T(8,128)(2,1)}, u32[]{:S(2)}) %copy-start.1) | copy-done | bytes 7077912
  31.9 0.0 copy-start.3
  31.9 1.1 %copy-done.3 = f32[776,256]{1,0:T(8,128)S(1)} copy-done((f32[776,256]{1,0:T(8,128)S(1)}, f32[776,256]{1,0:T(8,128)}, u32[]{:S(2)}) %copy-start.3) | copy-done | bytes 794648
  33.0 14.4 %pairs.1.parts_ref = f32[32,32,256]{2,1,0:T(8,128)S(1)} custom-call(s32[768]{0:T(1024)S(1)} %fusion.15.code_ref, bf16[96,288,128]{2,1,0:T(8,128)(2,1)S(1)} %copy-done.1, f32[96,32,256]{2,1,0:T(8,128)S(1)} %get-tuple-element.9.inv_ref, f32[776,256]{1,0:T(8,128)S(1)} %copy-done.3), custom_call_target="tpu_custom_call" | custom-call | tf_op jit(solution)/shard_map/pairs/pallas_call | solution.py:310
  47.4 18.0 %finish.1 = f32[16,64,128]{2,1,0:T(8,128)S(1)} custom-call(f32[32,32,256]{2,1,0:T(8,128)S(1)} %pairs.1.parts_ref), custom_call_target="tpu_custom_call" | custom-call | tf_op jit(solution)/shard_map/finish/pallas_call | solution.py:323
  65.5 1.0 %reshape.13 = f32[4,4,8192]{2,1,0:T(4,128)} reshape(f32[16,64,128]{2,1,0:T(8,128)S(1)} %finish.1) | data formatting | bytes 1048576 | tf_op jit(solution)/shard_map/reshape | solution.py:342
  (1 shorter events, 0.0 us)
Async XLA Ops:
  0.0 2.7 %copy-start.4 = (f32[8,24,200]{2,1,0:T(8,128)S(1)}, f32[8,24,200]{2,1,0:T(8,128)}, u32[]{:S(2)}) copy-start(f32[8,24,200]{2,1,0:T(8,128)} %param.7) | copy-start | bytes 460804
  0.0 2.7 %copy-start.5 = (s32[4]{0:T(128)S(1)}, s32[4]{0:T(128)}, u32[]{:S(2)}) copy-start(s32[4]{0:T(128)} %owner_ref.1) | copy-start | bytes 52
  0.0 28.6 %copy-start.6 = (s32[4,8,24]{2,1,0:T(8,128)S(1)}, s32[4,8,24]{2,1,0:T(8,128)}, u32[]{:S(2)}) copy-start(s32[4,8,24]{2,1,0:T(8,128)} %param.9) | copy-start | bytes 9220
  0.0 28.7 %copy-start.7 = (s32[96]{0:T(128)S(1)}, s32[96]{0:T(128)}, u32[]{:S(2)}) copy-start(s32[96]{0:T(128)} %param.6) | copy-start | bytes 1156
  24.8 2.9 %copy-start = (bf16[96,288,128]{2,1,0:T(8,128)(2,1)}, bf16[96,288,128]{2,1,0:T(8,128)(2,1)S(1)}, u32[]{:S(2)}) copy-start(bf16[96,288,128]{2,1,0:T(8,128)(2,1)S(1)} %get-tuple-element.8.z_ref) | copy-start | bytes 21233668
  27.7 0.9 %copy-start.2 = (f32[776,256]{1,0:T(8,128)}, f32[776,256]{1,0:T(8,128)S(1)}, u32[]{:S(2)}) copy-start(f32[776,256]{1,0:T(8,128)S(1)} %get-tuple-element.10.taps_ref) | copy-start | bytes 2383876
  28.9 3.0 %copy-start.1 = (bf16[96,288,128]{2,1,0:T(8,128)(2,1)S(1)}, bf16[96,288,128]{2,1,0:T(8,128)(2,1)}, u32[]{:S(2)}) copy-start(bf16[96,288,128]{2,1,0:T(8,128)(2,1)} %copy-done) | copy-start | bytes 21233668
  31.9 1.1 %copy-start.3 = (f32[776,256]{1,0:T(8,128)S(1)}, f32[776,256]{1,0:T(8,128)}, u32[]{:S(2)}) copy-start(f32[776,256]{1,0:T(8,128)} %copy-done.2) | copy-start | bytes 2383876

commit v2 on v1

--- a/solution.py
+++ b/solution.py
@@ -11,12 +11,68 @@
 offs = 32
 depth = 256
 rows_z = 288
-unroll = 32
+unroll = 16
 MESH = pl.DeviceIdType.MESH
 
 
+def pair_lists(steps, regions, region, order_ref, channels_ref, list_ref):
+    rows, used = channels_ref.shape
+    templates = rows // steps
+    per = templates // regions
+    held = steps * per
+    chans = order_ref.shape[1]
+    length = list_ref.shape[2]
+    f32, bf16 = jnp.float32, jnp.bfloat16
+    order = order_ref[...]
+    table = channels_ref[...]
+    hit = jnp.zeros((rows, chans), jnp.int32)
+    place = jnp.zeros((rows, chans), jnp.int32)
+    for j in range(used):
+        same = jnp.broadcast_to(table[:, j : j + 1], (rows, chans)) == order
+        hit = hit + jnp.where(same, 1, 0)
+        place = place + jnp.where(same, j, 0)
+    one = lax.broadcasted_iota(jnp.int32, (rows, rows), 0)
+    two = lax.broadcasted_iota(jnp.int32, (rows, rows), 1)
+    together = one % templates // per == two % templates // per
+
+    def ones(mask):
+        return jnp.where(mask, 1.0, 0.0).astype(bf16)
+
+    hits = hit.astype(f32)
+    rank = jnp.dot(ones(together & (two < one)), hits.astype(bf16), preferred_element_type=f32)
+    amount = jnp.dot(ones(together), hits.astype(bf16), preferred_element_type=f32)
+    entries = jnp.floor((amount + 1) * 0.5)
+    before = ones(lax.broadcasted_iota(jnp.int32, (chans, chans), 0) < lax.broadcasted_iota(jnp.int32, (chans, chans), 1))
+    first = jnp.dot(entries.astype(bf16), before, preferred_element_type=f32)
+    position = jnp.where(hits > 0, 2 * first + rank, -1.0)
+    row = lax.broadcasted_iota(jnp.int32, (rows, chans), 0)
+    step = row // templates
+    inner = row % templates * used + place
+    source = (inner // 16 * steps + step) * 16 + inner % 16
+    target = step * per + row % templates % per
+    column = lax.broadcasted_iota(jnp.int32, (rows, chans), 1)
+    empty = held * 2**17 + rows * used
+    code = (target * 2**17 + column * 2**10 + source - empty).astype(f32)
+    blank = jnp.zeros((rows, 128 - chans), f32)
+    position = jnp.concatenate([position, blank - 1], axis=1).T
+    code = jnp.concatenate([code, blank], axis=1).T
+    total = jnp.sum(entries, axis=1, keepdims=True)
+    for g in range(regions):
+        mine = [s * templates + g * per + k for s in range(steps) for k in range(per)]
+        for base in range(0, length, 128):
+            index = (lax.broadcasted_iota(jnp.int32, (128, 128), 1) + base).astype(f32)
+            found = jnp.zeros((128, 128), f32)
+            for t in mine:
+                found = found + jnp.where(position[:, t : t + 1] == index, code[:, t : t + 1], 0.0)
+            line = jnp.sum(found, axis=0, keepdims=True).astype(jnp.int32) + empty
+            if base + 128 == length:
+                last = lax.broadcasted_iota(jnp.int32, (1, 128), 1) == 127
+                line = jnp.where(last, total[mine[0] : mine[0] + 1].astype(jnp.int32), line)
+            list_ref[lax.rem(g - region - 1 + 2 * regions, regions), 0:1, base : base + 128] = line
+
+
 def prepare_kernel(
-    steps, count, owner_ref, library_ref, x_ref, edge_ref, z_ref, inv_ref, taps_ref,
+    steps, count, regions, owner_ref, library_ref, x_ref, edge_ref, order_ref, channels_ref, z_ref, inv_ref, taps_ref, list_ref,
     mine, got, sel, full, halo, halo_f, ext, halo_sems, one_send, one_recv, two_send, two_recv,
 ):
     me = lax.axis_index("tm")
@@ -96,11 +152,11 @@
 
         lax.fori_loop(first // width, last // width, group, 0)
 
+    pair_lists(steps, regions, region, order_ref, channels_ref, list_ref)
+
     edge_copy.wait()
     inside = (me < count - 1) & (lax.broadcasted_iota(jnp.int32, (chans, depth), 1) < taps - 1)
     halo_f[...] = jnp.where(inside, halo[...].astype(jnp.float32), 0.0)
-    split = chans // 3 // width * width
-    windows(0, split)
 
     for u in range(tiles):
         @pl.when(me != holders[u])
@@ -129,7 +185,7 @@
         for d in range(1, count):
             spread_copy(d).start()
 
-    windows(split, chans)
+    windows(0, chans)
 
     for u in range(tiles):
         @pl.when(me != holders[u])
@@ -148,81 +204,56 @@
             spread_copy(d).wait_send()
 
 
-def pair_kernel(code_ref, z_ref, inv_ref, taps_ref, out_ref, acc_ref, list_ref):
-    templates = out_ref.shape[0]
-
-    def compact(i, filled):
-        code = code_ref[i]
-        list_ref[filled] = code
-        return filled + jnp.where(code >= 0, 1, 0)
-
-    count = lax.fori_loop(0, code_ref.shape[0], compact, 0, unroll=8)
-    for u in range(unroll):
-        list_ref[count + u] = templates
+def pair_kernel(which, list_ref, z_ref, inv_ref, taps_ref, out_ref, acc_ref):
+    held = out_ref.shape[0]
+    total = list_ref[which, 0, list_ref.shape[2] - 1]
     acc_ref[...] = jnp.zeros_like(acc_ref)
 
-    def one_pair(code):
-        template = code & 63
-        col = (code >> 6) & 255
-        row = code >> 14
+    def shifted(row):
         base = jnp.broadcast_to(taps_ref[pl.ds(row, 1)], (8, depth))
         base = pltpu.roll(base, 0, 1, stride=1, stride_axis=0)
-        shifted = [base] + [pltpu.roll(base, a, 1) for a in range(8, offs, 8)]
-        matrix = jnp.concatenate(shifted, axis=0).astype(jnp.bfloat16)
+        return [base] + [pltpu.roll(base, a, 1) for a in range(8, offs, 8)]
+
+    def entry(e):
+        codes = [list_ref[which, 0, 2 * e + i] for i in range(2)]
+        matrix = jnp.concatenate(shifted(codes[0] & 1023) + shifted(codes[1] & 1023), axis=0).astype(jnp.bfloat16)
+        col = (codes[0] >> 10) & 127
         window = jnp.concatenate([z_ref[col, 0:depth], z_ref[col, offs : offs + depth]], axis=1)
         product = jnp.dot(matrix, window, preferred_element_type=jnp.float32)
-        return template, product * inv_ref[col]
+        scale = inv_ref[col]
+        return [(codes[i] >> 17, product[i * offs : (i + 1) * offs] * scale) for i in range(2)]
 
     def group(i, carry):
-        done = [one_pair(list_ref[i * unroll + u]) for u in range(unroll)]
-        for template, value in done:
-            acc_ref[template] += value
+        done = [entry(i * unroll + u) for u in range(unroll)]
+        for both in done:
+            for template, value in both:
+                acc_ref[template] += value
         return carry
 
-    lax.fori_loop(0, (count + unroll - 1) // unroll, group, 0)
-    out_ref[...] = acc_ref[:templates]
-
-
-def finish_kernel(total_time, steps, count, regions, parts_ref, out_ref, sent, arrived, stacked, power_sent, power_got, x_send, x_recv, p_send, p_recv):
+    lax.fori_loop(0, (total + unroll - 1) // unroll, group, 0)
+    out_ref[...] = acc_ref[:held].astype(out_ref.dtype)
+
+
+def finish_kernel(total_time, count, *refs):
+    *parts, out_ref, stacked, power_sent, power_got, p_send, p_recv = refs
     me = lax.axis_index("tm")
     region = lax.axis_index("region")
     barrier = pltpu.get_barrier_semaphore()
-    for d in range(1, regions):
-        pl.semaphore_signal(barrier, inc=1, device_id=(me, lax.rem(region + d, regions)), device_id_type=MESH)
     for d in range(1, count):
         pl.semaphore_signal(barrier, inc=1, device_id=(lax.rem(me + d, count), region), device_id_type=MESH)
     held = out_ref.shape[0]
-    per = held // steps
-
-    def chunk(d, s):
-        return pltpu.make_async_remote_copy(
-            src_ref=sent.at[d - 1, s], dst_ref=arrived.at[d - 1, s], send_sem=x_send.at[d - 1, s], recv_sem=x_recv.at[d - 1, s],
-            device_id=(me, lax.rem(region + d, regions)), device_id_type=MESH,
-        )
-
-    for s in range(steps):
-        for d in range(1, regions):
-            other = lax.rem(region + d, regions)
-            sent[d - 1, s] = parts_ref[pl.ds(other * held + s * per, per)].astype(jnp.bfloat16)
-        if s == 0:
-            pl.semaphore_wait(barrier, count - 1 + regions - 1)
-        for d in range(1, regions):
-            chunk(d, s).start()
     lane = lax.broadcasted_iota(jnp.int32, (1, 128), 1)
     power = jnp.zeros((1, 128), jnp.float32)
-    for s in range(steps):
-        for d in range(1, regions):
-            chunk(d, s).wait_recv()
-        for k in range(per):
-            at = s * per + k
-            value = parts_ref[region * held + at]
-            for d in range(1, regions):
-                value = value + arrived[d - 1, s, k].astype(jnp.float32)
-            total = jnp.sum(jnp.sum(value * value, axis=0, keepdims=True), axis=1, keepdims=True)
-            power = power + jnp.where(lane == at, total, 0.0)
-            upright = jnp.concatenate([value[:, :128], value[:, 128:]], axis=0).T
-            stacked[at] = jnp.concatenate([upright[:64], upright[64:]], axis=1)
+    for at in range(held):
+        value = parts[-1][at]
+        for other in parts[:-1]:
+            value = value + other[at].astype(jnp.float32)
+        total = jnp.sum(jnp.sum(value * value, axis=0, keepdims=True), axis=1, keepdims=True)
+        power = power + jnp.where(lane == at, total, 0.0)
+        upright = jnp.concatenate([value[:, :128], value[:, 128:]], axis=0).T
+        stacked[at] = jnp.concatenate([upright[:64], upright[64:]], axis=1)
     power_sent[...] = power
+    pl.semaphore_wait(barrier, count - 1)
     copies = []
     for d in range(1, count):
         copy = pltpu.make_async_remote_copy(
@@ -232,33 +263,12 @@
         copy.start()
         copies.append(copy)
     for copy in copies:
-        copy.wait_recv()
+        copy.wait()
     power = power + jnp.sum(power_got[...], axis=0)
     factor = lax.rsqrt(power / total_time + eps)
     for at in range(held):
         one = jnp.sum(jnp.where(lane == at, factor, 0.0), axis=1, keepdims=True)
         out_ref[at] = stacked[at] * one
-    for s in range(steps):
-        for d in range(1, regions):
-            chunk(d, s).wait_send()
-    for copy in copies:
-        copy.wait_send()
-
-
-def pair_list(station_order, channels, regions):
-    steps, templates, used = channels.shape
-    per = templates // regions
-    match = (channels.reshape(-1)[:, None] == station_order[None, :]).astype(jnp.int32)
-    local = jnp.sum(match, axis=1)
-    col = jnp.sum(match * jnp.arange(station_order.shape[0], dtype=jnp.int32)[None, :], axis=1)
-    pair = jnp.arange(steps * templates * used, dtype=jnp.int32)
-    step = pair // (templates * used)
-    inner = pair % (templates * used)
-    row = (inner // 16 * steps + step) * 16 + inner % 16
-    k = inner // used
-    template = (k // per) * (steps * per) + step * per + k % per
-    code = (row << 14) | (col << 6) | template
-    return jnp.where(local > 0, code, -1)
 
 
 def body(waveform, station_order, library, owner, channels):
@@ -274,20 +284,22 @@
     pairs = all_templates * used
     tiles = templates * used // 16
     lanes = time_local // offs
-    wide = 4
+    wide = 8
 
     vmem = pl.BlockSpec(memory_space=pltpu.VMEM)
     smem = pl.BlockSpec(memory_space=pltpu.SMEM)
     dma = pltpu.SemaphoreType.DMA
-    z, inv_scale, taps = pl.pallas_call(
-        functools.partial(prepare_kernel, steps, count),
+    length = -(-(held * used + chans + 2 * unroll + 1) // 128) * 128
+    z, inv_scale, taps, lists = pl.pallas_call(
+        functools.partial(prepare_kernel, steps, count, regions),
         out_shape=[
             jax.ShapeDtypeStruct((chans, rows_z, 128), jnp.bfloat16),
             jax.ShapeDtypeStruct((chans, offs, lanes), jnp.float32),
             jax.ShapeDtypeStruct((pairs + 8, depth), jnp.float32),
+            jax.ShapeDtypeStruct((regions, 1, length), jnp.int32),
         ],
-        in_specs=[smem, vmem, vmem, vmem],
-        out_specs=[vmem, vmem, vmem],
+        in_specs=[smem] + [vmem] * 5,
+        out_specs=[vmem] * 4,
         scratch_shapes=[
             pltpu.VMEM((tiles, 16, depth), jnp.bfloat16),
             pltpu.VMEM((count, 16, depth), jnp.bfloat16),
@@ -302,43 +314,46 @@
             dma((count - 1,)),
             dma((tiles,)),
         ],
-        compiler_params=pltpu.CompilerParams(collective_id=0, has_side_effects=True, vmem_limit_bytes=40 * 2**20),
+        compiler_params=pltpu.CompilerParams(collective_id=0, has_side_effects=True, vmem_limit_bytes=16 * 2**20),
         name="prepare",
-    )(owner, library.reshape(templates * used, tap_count), waveform.reshape(chans, blocks, 128), waveform[:, :depth])
-
-    codes = pair_list(station_order, channels, regions)
-    parts = pl.pallas_call(
-        pair_kernel,
-        out_shape=jax.ShapeDtypeStruct((all_templates, offs, lanes), jnp.float32),
-        in_specs=[smem, vmem, vmem, vmem],
+    )(
+        owner, library.reshape(templates * used, tap_count), waveform.reshape(chans, blocks, 128), waveform[:, :depth],
+        station_order.reshape(1, chans), channels.reshape(all_templates, used),
+    )
+
+    def partial_sums(which, dtype):
+        return pl.pallas_call(
+            functools.partial(pair_kernel, which),
+            out_shape=jax.ShapeDtypeStruct((held, offs, lanes), dtype),
+            in_specs=[smem, vmem, vmem, vmem],
+            out_specs=vmem,
+            scratch_shapes=[pltpu.VMEM((held + 1, offs, lanes), jnp.float32)],
+            compiler_params=pltpu.CompilerParams(vmem_limit_bytes=16 * 2**20),
+            cost_estimate=pl.CostEstimate(flops=held * used * offs * depth * lanes, bytes_accessed=12 * 2**20, transcendentals=0),
+            name="pairs",
+        )(lists, z, inv_scale, taps)
+
+    parts = []
+    for d in range(1, regions):
+        part = partial_sums(d - 1, jnp.bfloat16)
+        parts.append(lax.ppermute(part, "region", [(i, (i + d) % regions) for i in range(regions)]))
+    parts.append(partial_sums(regions - 1, jnp.float32))
+
+    result = pl.pallas_call(
+        functools.partial(finish_kernel, time_local * count, count),
+        out_shape=jax.ShapeDtypeStruct((held, blocks, 128), jnp.float32),
+        in_specs=[vmem] * regions,
         out_specs=vmem,
         scratch_shapes=[
-            pltpu.VMEM((all_templates + 1, offs, lanes), jnp.float32),
-            pltpu.SMEM((pairs + unroll,), jnp.int32),
-        ],
-        compiler_params=pltpu.CompilerParams(vmem_limit_bytes=40 * 2**20),
-        name="pairs",
-    )(codes, z, inv_scale, taps)
-
-    result = pl.pallas_call(
-        functools.partial(finish_kernel, time_local * count, steps, count, regions),
-        out_shape=jax.ShapeDtypeStruct((held, blocks, 128), jnp.float32),
-        in_specs=[vmem],
-        out_specs=vmem,
-        scratch_shapes=[
-            pltpu.VMEM((regions - 1, steps, per, offs, lanes), jnp.bfloat16),
-            pltpu.VMEM((regions - 1, steps, per, offs, lanes), jnp.bfloat16),
             pltpu.VMEM((held, blocks, 128), jnp.float32),
             pltpu.VMEM((1, 128), jnp.float32),
             pltpu.VMEM((count - 1, 1, 128), jnp.float32),
-            dma((regions - 1, steps)),
-            dma((regions - 1, steps)),
             dma((count - 1,)),
             dma((count - 1,)),
         ],
-        compiler_params=pltpu.CompilerParams(collective_id=1, has_side_effects=True, vmem_limit_bytes=40 * 2**20),
+        compiler_params=pltpu.CompilerParams(collective_id=1, has_side_effects=True, vmem_limit_bytes=16 * 2**20),
         name="finish",
-    )(parts)
+    )(*parts)
     return result.reshape(steps, per, time_local)
 
 

time: 66.8 us -> 49.3 us (0.74)
  Pallas kernels: 54.5 us -> 42.7 us
  local copies, waits for them, and re-layouts: 11.7 us -> 3.69 us
  starting transfers between devices: 0 us -> 1.55 us
  waiting for transfers between devices: 0 us -> 1.07 us
    pallas_call x3 -> x4, Pallas kernels: 54.5 us -> 42.7 us  [the longest x1 20.5 us: body(): pl.pallas_call(functools.partial(prepare_kernel, steps, count, regions),...]
    unnamed x17 -> x9, local copies, waits for them, and re-layouts: 9.79 us -> 1.84 us
    ppermute x0 -> x1, starting transfers between devices: none -> 1.55 us  [body(): lax.ppermute(part, 'region', [(i, (i + d) % regions) for i in range(regio...]
    ppermute x0 -> x1, waiting for transfers between devices: none -> 1.07 us  [body(): lax.ppermute(part, 'region', [(i, (i + d) % regions) for i in range(regio...]
  transfers between devices with their start and end apart: 0 -> 1, of which waited for: 0 -> 1; matrix products, arithmetic and copies ran while one was open for 0% -> 0% of each run, Pallas kernels for 0% -> 13%
where the time goes in v2:
time: 49.3 us; the launch traced here: 49.1 us
  Pallas kernels  42.7 us (87%)
  local copies, waits for them, and re-layouts  3.69 us (7%)
  starting transfers between devices  1.55 us (3%)
  waiting for transfers between devices  1.07 us (2%)
    pallas_call x1, Pallas kernels, body(): pl.pallas_call(functools.partial(prepare_kernel, steps, count, regions),...  20.5 us
    pallas_call x2, Pallas kernels, partial_sums(): pl.pallas_call(functools.partial(pair_kernel, which), out_shape=jax.Shape...  12.7 us
    pallas_call x1, Pallas kernels, body(): pl.pallas_call(functools.partial(finish_kernel, time_local * count, count...  9.47 us
    unnamed x9, local copies, waits for them, and re-layouts  1.84 us
    ppermute x1, starting transfers between devices, body(): lax.ppermute(part, 'region', [(i, (i + d) % regions) for i in range(regio...  1.55 us
    ppermute x1, waiting for transfers between devices, body(): lax.ppermute(part, 'region', [(i, (i + d) % regions) for i in range(regio...  1.07 us
    reshape x1, local copies, waits for them, and re-layouts, body(): return result.reshape(steps, per, time_local)  1.01 us
  transfers between devices with their start and end apart: 1, of which 1 were waited for; matrix products, arithmetic and copies ran while one was open for 0% of the time, Pallas kernels for 13%

profile of v2, /device:TPU:0, one launch (start us, length us, event | category | flops | bytes accessed | tf_op | source)
XLA Modules:
  0.0 49.1 jit_solution(3309593276764517991)
XLA Ops:
  0.0 0.0 copy-start.1
  0.0 0.0 copy-start.2
  0.0 0.0 copy-start
  0.0 0.0 copy-start.3
  0.0 0.8 %slice.3.edge_ref = bf16[96,256]{1,0:T(8,128)(2,1)S(1)} slice(bf16[96,8192]{1,0:T(8,128)(2,1)} %param.5), slice={[0:96], [0:256]} | slice | bytes 98304 | tf_op jit(solution)/shard_map/slice | solution.py:320
  0.9 1.8 %copy.6 = bf16[12,8,64,128]{3,2,1,0:T(8,128)(2,1)S(1)} copy(bf16[12,8,64,128]{3,1,2,0:T(8,128)(2,1)} %bitcast.9) | data formatting | bytes 3145728
  2.7 0.0 copy-done.1
  2.7 0.0 copy-done.2
  2.7 0.0 copy-done
  2.7 0.0 copy-done.3
  2.7 20.5 %prepare.1 = (bf16[96,288,128]{2,1,0:T(8,128)(2,1)S(1)}, f32[96,32,256]{2,1,0:T(8,128)S(1)}, f32[776,256]{1,0:T(8,128)S(1)}, s32[2,1,640]{2,1,0:T(1,128)S(1)}) custom-call(s32[4]{0:T(128)S(1)} %copy-done.2, f32[192,200]{1,0:T(8,128)S(1)} %bitcast.6, bf16[96,64,128]{2,1,0:T(8,128)(2,1)S(1)} %bitcast.5, bf16[96,256]{1,0:T(8,128)(2,1)S(1)} %slice.3.edge_ref, ...), custom_call_target="tpu_custom_call" | custom-call | tf_op jit(solution)/shard_map/prepare/pallas_call | solution.py:293
  23.3 6.4 %pairs.2 = bf16[16,32,256]{2,1,0:T(8,128)(2,1)S(1)} custom-call(s32[2,1,640]{2,1,0:T(1,128)S(1)} %get-tuple-element.9.list_ref, bf16[96,288,128]{2,1,0:T(8,128)(2,1)S(1)} %get-tuple-element.10.z_ref, f32[96,32,256]{2,1,0:T(8,128)S(1)} %get-tuple-element.11.inv_ref, f32[776,256]{1,0:T(8,128)S(1)} %get-tuple-element.12.taps_ref), custom_call_target="tpu_custom_call" | custom-call | flops 805306368 | bytes 12582912 | tf_op jit(solution)/shard_map/pairs/pallas_call | solution.py:325
  29.7 1.5 %collective-permute-start = (bf16[16,32,256]{2,1,0:T(8,128)(2,1)S(1)}, bf16[16,32,256]{2,1,0:T(8,128)(2,1)S(1)}, u32[]{:S(2)}, u32[]{:S(2)}) collective-permute-start(bf16[16,32,256]{2,1,0:T(8,128)(2,1)S(1)} %pairs.2), channel_id=1, source_target_pairs={{0,1},{1,0},{2,3},{3,2},{4,5},{5,4},{6,7},{7,6},{8,9},{9,8},{10,11... | collective-permute-start | bytes 786440 | tf_op jit(solution)/shard_map/ppermute | solution.py:339
  31.2 6.4 %pairs.3.refs_1_ = f32[16,32,256]{2,1,0:T(8,128)S(1)} custom-call(s32[2,1,640]{2,1,0:T(1,128)S(1)} %get-tuple-element.9.list_ref, bf16[96,288,128]{2,1,0:T(8,128)(2,1)S(1)} %get-tuple-element.10.z_ref, f32[96,32,256]{2,1,0:T(8,128)S(1)} %get-tuple-element.11.inv_ref, f32[776,256]{1,0:T(8,128)S(1)} %get-tuple-element.12.taps_ref), custom_call_target="tpu_custom_call" | custom-call | flops 805306368 | bytes 12582912 | tf_op jit(solution)/shard_map/pairs/pallas_call | solution.py:325
  37.6 1.1 %collective-permute-done.refs_0_ = bf16[16,32,256]{2,1,0:T(8,128)(2,1)S(1)} collective-permute-done((bf16[16,32,256]{2,1,0:T(8,128)(2,1)S(1)}, bf16[16,32,256]{2,1,0:T(8,128)(2,1)S(1)}, u32[]{:S(2)}, u32[]{:S(2)}) %collective-permute-start) | collective-permute-done | bytes 262176 | tf_op jit(solution)/shard_map/ppermute | solution.py:339
  38.6 9.5 %finish.1 = f32[16,64,128]{2,1,0:T(8,128)S(1)} custom-call(bf16[16,32,256]{2,1,0:T(8,128)(2,1)S(1)} %collective-permute-done.refs_0_, f32[16,32,256]{2,1,0:T(8,128)S(1)} %pairs.3.refs_1_), custom_call_target="tpu_custom_call" | custom-call | tf_op jit(solution)/shard_map/finish/pallas_call | solution.py:342
  48.1 1.0 %reshape.19 = f32[4,4,8192]{2,1,0:T(4,128)} reshape(f32[16,64,128]{2,1,0:T(8,128)S(1)} %finish.1) | data formatting | bytes 1048576 | tf_op jit(solution)/shard_map/reshape | solution.py:357
Async XLA Ops:
  0.0 2.7 %copy-start.1 = (s32[4,8,24]{2,1,0:T(8,128)S(1)}, s32[4,8,24]{2,1,0:T(8,128)}, u32[]{:S(2)}) copy-start(s32[4,8,24]{2,1,0:T(8,128)} %param.9) | copy-start | bytes 9220
  0.0 2.7 %copy-start.2 = (s32[4]{0:T(128)S(1)}, s32[4]{0:T(128)}, u32[]{:S(2)}) copy-start(s32[4]{0:T(128)} %owner_ref.1) | copy-start | bytes 52
  0.0 2.7 %copy-start = (f32[8,24,200]{2,1,0:T(8,128)S(1)}, f32[8,24,200]{2,1,0:T(8,128)}, u32[]{:S(2)}) copy-start(f32[8,24,200]{2,1,0:T(8,128)} %param.7) | copy-start | bytes 460804
  0.0 2.7 %copy-start.3 = (s32[96]{0:T(128)S(1)}, s32[96]{0:T(128)}, u32[]{:S(2)}) copy-start(s32[96]{0:T(128)} %param.6) | copy-start | bytes 1156
  29.7 9.0 %collective-permute-start = (bf16[16,32,256]{2,1,0:T(8,128)(2,1)S(1)}, bf16[16,32,256]{2,1,0:T(8,128)(2,1)S(1)}, u32[]{:S(2)}, u32[]{:S(2)}) collective-permute-start(bf16[16,32,256]{2,1,0:T(8,128)(2,1)S(1)} %pairs.2), channel_id=1, source_target_pairs={{0,1},{1,0},{2,3},{3,2},{4,5},{5,4},{6,7},{7,6},{8,9},{9,8},{10,11... | collective-permute-start | bytes 786440 | tf_op jit(solution)/shard_map/ppermute | solution.py:339

commit v3 on v2

--- a/solution.py
+++ b/solution.py
@@ -11,7 +11,7 @@
 offs = 32
 depth = 256
 rows_z = 288
-unroll = 16
+unroll = 32
 MESH = pl.DeviceIdType.MESH
 
 
@@ -72,14 +72,26 @@
 
 
 def prepare_kernel(
-    steps, count, regions, owner_ref, library_ref, x_ref, edge_ref, order_ref, channels_ref, z_ref, inv_ref, taps_ref, list_ref,
-    mine, got, sel, full, halo, halo_f, ext, halo_sems, one_send, one_recv, two_send, two_recv,
+    steps, count, regions, owner_hbm, library_hbm, x_ref, order_hbm, channels_hbm, z_ref, inv_ref, taps_ref, list_ref,
+    owner_ref, library_ref, order_ref, channels_ref, small_sems, mine, got, sel, full, halo, local, ext, local_sem, halo_sems, one_send, one_recv, two_send, two_recv, pass_send,
 ):
     me = lax.axis_index("tm")
     region = lax.axis_index("region")
     barrier = pltpu.get_barrier_semaphore()
     for d in range(1, count):
         pl.semaphore_signal(barrier, inc=1, device_id=(lax.rem(me + d, count), region), device_id_type=MESH)
+    small = [
+        pltpu.make_async_copy(source, target, small_sems.at[i])
+        for i, (source, target) in enumerate(
+            [(library_hbm, library_ref), (owner_hbm, owner_ref), (order_hbm, order_ref), (channels_hbm, channels_ref)]
+        )
+    ]
+    for copy in small:
+        copy.start()
+    load = pltpu.make_async_copy(x_ref, local, local_sem)
+    load.start()
+    for copy in small:
+        copy.wait()
 
     taps = library_ref.shape[1]
     tiles = mine.shape[0]
@@ -89,15 +101,21 @@
     normed = jnp.concatenate([normed, jnp.zeros((panel.shape[0], depth - taps), jnp.float32)], axis=1)
     mine[...] = normed.astype(jnp.bfloat16).reshape(tiles, 16, depth)
 
-    holders = [u * count // tiles for u in range(tiles)]
-    my_tile = (me * tiles + count - 1) // count
-    holding = my_tile * count // tiles == me
-    my_tile = jnp.minimum(my_tile, tiles - 1)
+    half = tiles // 2
+    chips = count // 2
+    chip = me // 2
+    core = me % 2
+    sibling = chip * 2 + 1 - core
+    seats = [v * chips // half for v in range(half)]
+    holders = [seats[u // 2] * 2 + u % 2 for u in range(tiles)]
+    seat = (chip * half + chips - 1) // chips
+    holding = seat * chips // half == chip
+    my_tile = jnp.minimum(seat, half - 1) * 2 + core
 
     pl.semaphore_wait(barrier, count - 1)
     left = lax.rem(me + count - 1, count)
     edge_copy = pltpu.make_async_remote_copy(
-        src_ref=edge_ref, dst_ref=halo, send_sem=halo_sems.at[0], recv_sem=halo_sems.at[1],
+        src_ref=x_ref.at[:, pl.ds(0, depth)], dst_ref=halo, send_sem=halo_sems.at[0], recv_sem=halo_sems.at[1],
         device_id=(left, region), device_id_type=MESH,
     )
     edge_copy.start()
@@ -113,19 +131,16 @@
         def _():
             piece(u).start()
 
-    chans, blocks, _ = x_ref.shape
+    chans = x_ref.shape[0]
+    blocks = x_ref.shape[1] // 128
     lane = lax.broadcasted_iota(jnp.int32, (1, 128), 1)
     low_half = lane < 64
     spread = lax.broadcasted_iota(jnp.int32, (offs, depth), 1) - lax.broadcasted_iota(jnp.int32, (offs, depth), 0)
     band = ((spread >= 0) & (spread < taps)).astype(jnp.float32).astype(jnp.bfloat16)
-    width = ext.shape[0]
-
-    def channel(c, slot):
-        ext[slot, 0:blocks] = x_ref[c].astype(jnp.float32)
-        rim = halo_f[pl.ds(c, 1), :]
-        ext[slot, blocks : blocks + 1] = rim[:, 0:128]
-        ext[slot, blocks + 1 : blocks + 2] = rim[:, 128:256]
-        x = [ext[slot, m : m + blocks] for m in range(3)]
+    width = 8
+
+    def channel(c):
+        x = [ext[c, m : m + blocks] for m in range(3)]
         y = [pltpu.roll(v, 64, 1) for v in x]
         columns = []
         for m in range(3):
@@ -147,26 +162,43 @@
     def windows(first, last):
         def group(i, carry):
             for slot in range(width):
-                channel(i * width + slot, slot)
+                channel(i * width + slot)
             return carry
 
         lax.fori_loop(first // width, last // width, group, 0)
 
     pair_lists(steps, regions, region, order_ref, channels_ref, list_ref)
-
+    load.wait()
+
+    def lay_out(i, carry):
+        at = pl.ds(pl.multiple_of(i * 16, 16), 16)
+        ext[at, 0:blocks] = local[at, :].astype(jnp.float32).reshape(16, blocks, 128)
+        return carry
+
+    lax.fori_loop(0, chans // 16, lay_out, 0)
+    rest = chans // 16 * 16
+    if rest < chans:
+        ext[rest:chans, 0:blocks] = local[rest:chans, :].astype(jnp.float32).reshape(chans - rest, blocks, 128)
     edge_copy.wait()
-    inside = (me < count - 1) & (lax.broadcasted_iota(jnp.int32, (chans, depth), 1) < taps - 1)
-    halo_f[...] = jnp.where(inside, halo[...].astype(jnp.float32), 0.0)
+    inside = (me < count - 1) & (lax.broadcasted_iota(jnp.int32, (1, depth), 1) < taps - 1)
+    for i in range(0, chans, 16):
+        end = min(i + 16, chans)
+        rim = jnp.where(inside, halo[i:end].astype(jnp.float32), 0.0)
+        ext[i:end, blocks : blocks + 2] = rim.reshape(end - i, 2, 128)
+    early = chans // 4 // width * width
+    late = chans * 3 // 4 // width * width
+    windows(0, early)
 
     for u in range(tiles):
         @pl.when(me != holders[u])
         def _():
             piece(u).wait_send()
 
-    def spread_copy(d):
+    def spread_copy(e):
+        peer = sibling if e == 0 else lax.rem(chip + e, chips) * 2 + core
         return pltpu.make_async_remote_copy(
-            src_ref=sel, dst_ref=full.at[my_tile], send_sem=two_send.at[d - 1], recv_sem=two_recv.at[my_tile],
-            device_id=(lax.rem(me + d, count), region), device_id_type=MESH,
+            src_ref=sel, dst_ref=full.at[my_tile], send_sem=two_send.at[e], recv_sem=two_recv.at[my_tile],
+            device_id=(peer, region), device_id_type=MESH,
         )
 
     @pl.when(holding)
@@ -182,26 +214,46 @@
         for s in range(steps):
             sel[s] = got[owner_ref[s]]
         full[my_tile] = sel[...]
-        for d in range(1, count):
-            spread_copy(d).start()
-
-    windows(0, chans)
-
-    for u in range(tiles):
-        @pl.when(me != holders[u])
+        for e in range(1, chips):
+            spread_copy(e).start()
+        spread_copy(0).start()
+
+    windows(early, late)
+
+    def pass_copy(v):
+        u = 2 * v + core
+        return pltpu.make_async_remote_copy(
+            src_ref=full.at[u], dst_ref=full.at[u], send_sem=pass_send.at[v], recv_sem=two_recv.at[u],
+            device_id=(sibling, region), device_id_type=MESH,
+        )
+
+    for v in range(half):
+        @pl.when(chip != seats[v])
         def _():
-            pltpu.make_async_remote_copy(
-                src_ref=sel, dst_ref=full.at[u], send_sem=two_send.at[0], recv_sem=two_recv.at[u],
-                device_id=(left, region), device_id_type=MESH,
-            ).wait_recv()
+            pass_copy(v).wait_recv()
+            pass_copy(v).start()
+
+    windows(late, chans)
+
+    for v in range(half):
+        u = 2 * v + 1 - core
+        pltpu.make_async_remote_copy(
+            src_ref=sel, dst_ref=full.at[u], send_sem=two_send.at[0], recv_sem=two_recv.at[u],
+            device_id=(sibling, region), device_id_type=MESH,
+        ).wait_recv()
 
     taps_ref[0 : tiles * steps * 16] = full[...].astype(jnp.float32).reshape(tiles * steps * 16, depth)
     taps_ref[tiles * steps * 16 :] = jnp.zeros((8, depth), jnp.float32)
 
     @pl.when(holding)
     def _():
-        for d in range(1, count):
-            spread_copy(d).wait_send()
+        for e in range(chips):
+            spread_copy(e).wait_send()
+
+    for v in range(half):
+        @pl.when(chip != seats[v])
+        def _():
+            pass_copy(v).wait_send()
 
 
 def pair_kernel(which, list_ref, z_ref, inv_ref, taps_ref, out_ref, acc_ref):
@@ -210,13 +262,12 @@
     acc_ref[...] = jnp.zeros_like(acc_ref)
 
     def shifted(row):
-        base = jnp.broadcast_to(taps_ref[pl.ds(row, 1)], (8, depth))
-        base = pltpu.roll(base, 0, 1, stride=1, stride_axis=0)
-        return [base] + [pltpu.roll(base, a, 1) for a in range(8, offs, 8)]
+        base = jnp.broadcast_to(taps_ref[pl.ds(row, 1)], (offs, depth))
+        return pltpu.roll(base, 0, 1, stride=1, stride_axis=0)
 
     def entry(e):
         codes = [list_ref[which, 0, 2 * e + i] for i in range(2)]
-        matrix = jnp.concatenate(shifted(codes[0] & 1023) + shifted(codes[1] & 1023), axis=0).astype(jnp.bfloat16)
+        matrix = jnp.concatenate([shifted(codes[i] & 1023) for i in range(2)], axis=0).astype(jnp.bfloat16)
         col = (codes[0] >> 10) & 127
         window = jnp.concatenate([z_ref[col, 0:depth], z_ref[col, offs : offs + depth]], axis=1)
         product = jnp.dot(matrix, window, preferred_element_type=jnp.float32)
@@ -248,10 +299,9 @@
         value = parts[-1][at]
         for other in parts[:-1]:
             value = value + other[at].astype(jnp.float32)
+        stacked[at] = value
         total = jnp.sum(jnp.sum(value * value, axis=0, keepdims=True), axis=1, keepdims=True)
         power = power + jnp.where(lane == at, total, 0.0)
-        upright = jnp.concatenate([value[:, :128], value[:, 128:]], axis=0).T
-        stacked[at] = jnp.concatenate([upright[:64], upright[64:]], axis=1)
     power_sent[...] = power
     pl.semaphore_wait(barrier, count - 1)
     copies = []
@@ -262,13 +312,17 @@
         )
         copy.start()
         copies.append(copy)
+    for at in range(held):
+        value = stacked[at]
+        turned = jnp.concatenate([value[:, :128], value[:, 128:]], axis=0).T
+        out_ref[at] = jnp.concatenate([turned[:64], turned[64:]], axis=1)
     for copy in copies:
         copy.wait()
     power = power + jnp.sum(power_got[...], axis=0)
     factor = lax.rsqrt(power / total_time + eps)
     for at in range(held):
         one = jnp.sum(jnp.where(lane == at, factor, 0.0), axis=1, keepdims=True)
-        out_ref[at] = stacked[at] * one
+        out_ref[at] = out_ref[at] * one
 
 
 def body(waveform, station_order, library, owner, channels):
@@ -284,7 +338,6 @@
     pairs = all_templates * used
     tiles = templates * used // 16
     lanes = time_local // offs
-    wide = 8
 
     vmem = pl.BlockSpec(memory_space=pltpu.VMEM)
     smem = pl.BlockSpec(memory_space=pltpu.SMEM)
@@ -298,28 +351,35 @@
             jax.ShapeDtypeStruct((pairs + 8, depth), jnp.float32),
             jax.ShapeDtypeStruct((regions, 1, length), jnp.int32),
         ],
-        in_specs=[smem] + [vmem] * 5,
+        in_specs=[pl.BlockSpec(memory_space=pltpu.HBM)] * 5,
         out_specs=[vmem] * 4,
         scratch_shapes=[
+            pltpu.SMEM((steps,), jnp.int32),
+            pltpu.VMEM((templates * used, tap_count), jnp.float32),
+            pltpu.VMEM((1, chans), jnp.int32),
+            pltpu.VMEM((all_templates, used), jnp.int32),
+            dma((4,)),
             pltpu.VMEM((tiles, 16, depth), jnp.bfloat16),
             pltpu.VMEM((count, 16, depth), jnp.bfloat16),
             pltpu.VMEM((steps, 16, depth), jnp.bfloat16),
             pltpu.VMEM((tiles, steps, 16, depth), jnp.bfloat16),
             pltpu.VMEM((chans, depth), jnp.bfloat16),
-            pltpu.VMEM((chans, depth), jnp.float32),
-            pltpu.VMEM((wide, blocks + 8, 128), jnp.float32),
+            pltpu.VMEM((chans, time_local), jnp.bfloat16),
+            pltpu.VMEM((chans, blocks + 8, 128), jnp.float32),
+            dma,
             dma((2,)),
             dma((tiles,)),
             dma((count,)),
-            dma((count - 1,)),
+            dma((count // 2,)),
             dma((tiles,)),
+            dma((tiles // 2,)),
         ],
         compiler_params=pltpu.CompilerParams(collective_id=0, has_side_effects=True, vmem_limit_bytes=16 * 2**20),
         name="prepare",
-    )(
-        owner, library.reshape(templates * used, tap_count), waveform.reshape(chans, blocks, 128), waveform[:, :depth],
+    )(*[pltpu.with_memory_space_constraint(v, pltpu.HBM) for v in (
+        owner, library.reshape(templates * used, tap_count), waveform,
         station_order.reshape(1, chans), channels.reshape(all_templates, used),
-    )
+    )])
 
     def partial_sums(which, dtype):
         return pl.pallas_call(
@@ -345,7 +405,7 @@
         in_specs=[vmem] * regions,
         out_specs=vmem,
         scratch_shapes=[
-            pltpu.VMEM((held, blocks, 128), jnp.float32),
+            pltpu.VMEM((held, offs, lanes), jnp.float32),
             pltpu.VMEM((1, 128), jnp.float32),
             pltpu.VMEM((count - 1, 1, 128), jnp.float32),
             dma((count - 1,)),

time: 49.3 us -> 42.2 us (0.86)
  Pallas kernels: 42.7 us -> 36.2 us
  local copies, waits for them, and re-layouts: 3.69 us -> 1.01 us
  waiting for transfers between devices: 1.07 us -> 3.27 us
    pallas_call x2, Pallas kernels: 12.7 us -> 8.77 us  [partial_sums(): pl.pallas_call(functools.partial(pair_kernel, which), out_shape=jax.Shape...]
    pallas_call x1, Pallas kernels: 9.47 us -> 7 us  [body(): pl.pallas_call(functools.partial(finish_kernel, time_local * count, count...]
    ppermute x1, waiting for transfers between devices: 1.07 us -> 3.27 us  [body(): lax.ppermute(part, 'region', [(i, (i + d) % regions) for i in range(regio...]
    unnamed x9 -> x0, local copies, waits for them, and re-layouts: 1.84 us -> none
    slice x1 -> x0, local copies, waits for them, and re-layouts: 0.84 us -> none  [body(): waveform[:, :depth]]
  transfers between devices with their start and end apart: 1 -> 1, of which waited for: 1 -> 1; matrix products, arithmetic and copies ran while one was open for 0% -> 0% of each run, Pallas kernels for 13% -> 10%
where the time goes in v3:
time: 42.2 us; the launch traced here: 42 us
  Pallas kernels  36.2 us (86%)
  waiting for transfers between devices  3.27 us (8%)
  starting transfers between devices  1.54 us (4%)
  local copies, waits for them, and re-layouts  1.01 us (2%)
    pallas_call x1, Pallas kernels, body(): pl.pallas_call(functools.partial(prepare_kernel, steps, count, regions),...  20.4 us
    pallas_call x2, Pallas kernels, partial_sums(): pl.pallas_call(functools.partial(pair_kernel, which), out_shape=jax.Shape...  8.77 us
    pallas_call x1, Pallas kernels, body(): pl.pallas_call(functools.partial(finish_kernel, time_local * count, count...  7 us
    ppermute x1, waiting for transfers between devices, body(): lax.ppermute(part, 'region', [(i, (i + d) % regions) for i in range(regio...  3.27 us
    ppermute x1, starting transfers between devices, body(): lax.ppermute(part, 'region', [(i, (i + d) % regions) for i in range(regio...  1.54 us
    reshape x1, local copies, waits for them, and re-layouts, body(): return result.reshape(steps, per, time_local)  1.01 us
  transfers between devices with their start and end apart: 1, of which 1 were waited for; matrix products, arithmetic and copies ran while one was open for 0% of the time, Pallas kernels for 10%

profile of v3, /device:TPU:0, one launch (start us, length us, event | category | flops | bytes accessed | tf_op | source)
XLA Modules:
  0.0 42.0 jit_solution(18424892912253194766)
XLA Ops:
  0.0 20.4 %prepare.1 = (bf16[96,288,128]{2,1,0:T(8,128)(2,1)S(1)}, f32[96,32,256]{2,1,0:T(8,128)S(1)}, f32[776,256]{1,0:T(8,128)S(1)}, s32[2,1,640]{2,1,0:T(1,128)S(1)}) custom-call(s32[4]{0:T(128)} %owner_hbm.1, f32[192,200]{1,0:T(8,128)} %bitcast.3, bf16[96,8192]{1,0:T(8,128)(2,1)} %x_ref.1, s32[1,96]{1,0:T(1,128)} %bitcast.5, s32[32,24]{1,0:T(8,128)} %bitcast.4), custom_call_target="tpu_custom_call" | custom-call | tf_op jit(solution)/shard_map/prepare/pallas_call | solution.py:346
  20.4 4.4 %pairs.2 = bf16[16,32,256]{2,1,0:T(8,128)(2,1)S(1)} custom-call(s32[2,1,640]{2,1,0:T(1,128)S(1)} %get-tuple-element.9.list_ref, bf16[96,288,128]{2,1,0:T(8,128)(2,1)S(1)} %get-tuple-element.10.z_ref, f32[96,32,256]{2,1,0:T(8,128)S(1)} %get-tuple-element.11.inv_ref, f32[776,256]{1,0:T(8,128)S(1)} %get-tuple-element.12.taps_ref), custom_call_target="tpu_custom_call" | custom-call | flops 805306368 | bytes 12582912 | tf_op jit(solution)/shard_map/pairs/pallas_call | solution.py:385
  24.8 1.5 %collective-permute-start = (bf16[16,32,256]{2,1,0:T(8,128)(2,1)S(1)}, bf16[16,32,256]{2,1,0:T(8,128)(2,1)S(1)}, u32[]{:S(2)}, u32[]{:S(2)}) collective-permute-start(bf16[16,32,256]{2,1,0:T(8,128)(2,1)S(1)} %pairs.2), channel_id=1, source_target_pairs={{0,1},{1,0},{2,3},{3,2},{4,5},{5,4},{6,7},{7,6},{8,9},{9,8},{10,11... | collective-permute-start | bytes 786440 | tf_op jit(solution)/shard_map/ppermute | solution.py:399
  26.4 4.4 %pairs.3.refs_1_ = f32[16,32,256]{2,1,0:T(8,128)S(1)} custom-call(s32[2,1,640]{2,1,0:T(1,128)S(1)} %get-tuple-element.9.list_ref, bf16[96,288,128]{2,1,0:T(8,128)(2,1)S(1)} %get-tuple-element.10.z_ref, f32[96,32,256]{2,1,0:T(8,128)S(1)} %get-tuple-element.11.inv_ref, f32[776,256]{1,0:T(8,128)S(1)} %get-tuple-element.12.taps_ref), custom_call_target="tpu_custom_call" | custom-call | flops 805306368 | bytes 12582912 | tf_op jit(solution)/shard_map/pairs/pallas_call | solution.py:385
  30.8 3.3 %collective-permute-done.refs_0_ = bf16[16,32,256]{2,1,0:T(8,128)(2,1)S(1)} collective-permute-done((bf16[16,32,256]{2,1,0:T(8,128)(2,1)S(1)}, bf16[16,32,256]{2,1,0:T(8,128)(2,1)S(1)}, u32[]{:S(2)}, u32[]{:S(2)}) %collective-permute-start) | collective-permute-done | bytes 262176 | tf_op jit(solution)/shard_map/ppermute | solution.py:399
  34.0 7.0 %finish.1 = f32[16,64,128]{2,1,0:T(8,128)S(1)} custom-call(bf16[16,32,256]{2,1,0:T(8,128)(2,1)S(1)} %collective-permute-done.refs_0_, f32[16,32,256]{2,1,0:T(8,128)S(1)} %pairs.3.refs_1_), custom_call_target="tpu_custom_call" | custom-call | tf_op jit(solution)/shard_map/finish/pallas_call | solution.py:402
  41.0 1.0 %reshape.15 = f32[4,4,8192]{2,1,0:T(4,128)} reshape(f32[16,64,128]{2,1,0:T(8,128)S(1)} %finish.1) | data formatting | bytes 1048576 | tf_op jit(solution)/shard_map/reshape | solution.py:417
Async XLA Ops:
  24.8 9.2 %collective-permute-start = (bf16[16,32,256]{2,1,0:T(8,128)(2,1)S(1)}, bf16[16,32,256]{2,1,0:T(8,128)(2,1)S(1)}, u32[]{:S(2)}, u32[]{:S(2)}) collective-permute-start(bf16[16,32,256]{2,1,0:T(8,128)(2,1)S(1)} %pairs.2), channel_id=1, source_target_pairs={{0,1},{1,0},{2,3},{3,2},{4,5},{5,4},{6,7},{7,6},{8,9},{9,8},{10,11... | collective-permute-start | bytes 786440 | tf_op jit(solution)/shard_map/ppermute | solution.py:399

commit v4 on v3

--- a/solution.py
+++ b/solution.py
@@ -73,7 +73,7 @@
 
 def prepare_kernel(
     steps, count, regions, owner_hbm, library_hbm, x_ref, order_hbm, channels_hbm, z_ref, inv_ref, taps_ref, list_ref,
-    owner_ref, library_ref, order_ref, channels_ref, small_sems, mine, got, sel, full, halo, local, ext, local_sem, halo_sems, one_send, one_recv, two_send, two_recv, pass_send,
+    owner_ref, library_ref, order_ref, channels_ref, small_sems, mine, got, sel, full, halo, local, ext, turned, local_sem, halo_sems, one_send, one_recv, two_send, two_recv, pass_send,
 ):
     me = lax.axis_index("tm")
     region = lax.axis_index("region")
@@ -137,16 +137,18 @@
     low_half = lane < 64
     spread = lax.broadcasted_iota(jnp.int32, (offs, depth), 1) - lax.broadcasted_iota(jnp.int32, (offs, depth), 0)
     band = ((spread >= 0) & (spread < taps)).astype(jnp.float32).astype(jnp.bfloat16)
-    width = 8
-
-    def channel(c):
-        x = [ext[c, m : m + blocks] for m in range(3)]
-        y = [pltpu.roll(v, 64, 1) for v in x]
-        columns = []
-        for m in range(3):
-            second = jnp.where(low_half, y[m], y[m + 1]) if m < 2 else y[m]
-            columns.append(jnp.concatenate([x[m], second], axis=0).T)
-        z = jnp.concatenate([columns[0], columns[1], columns[2][: rows_z - 256]], axis=0)
+    width = 16 if chans % 16 == 0 else 8
+
+    def channel(c, tips):
+        y = [turned[c, m : m + blocks] for m in range(3)]
+        columns = [
+            jnp.concatenate([ext[c, m : m + blocks], jnp.where(low_half, y[m], y[m + 1])], axis=0).T for m in range(2)
+        ]
+        last = pltpu.roll(columns[0][:8], 126, 1)
+        last = jnp.where(lane % 64 == 62, pltpu.roll(columns[1][:8], 127, 1), last)
+        last = jnp.where(lane == 63, pltpu.roll(tips[0], lax.rem(191 - c, 128), 1), last)
+        last = jnp.where(lane == 127, pltpu.roll(tips[1], 127 - c, 1), last)
+        z = jnp.concatenate(columns + [last, jnp.zeros((rows_z - 264, 128), jnp.float32)], axis=0)
         z_ref[c] = z.astype(jnp.bfloat16)
         square = z * z
         high = square.astype(jnp.bfloat16)
@@ -159,10 +161,10 @@
         energy = energy + jnp.dot(band, both(low), preferred_element_type=jnp.float32)
         inv_ref[c] = lax.rsqrt(energy + taps * water_level)
 
-    def windows(first, last):
+    def windows(first, last, tips):
         def group(i, carry):
             for slot in range(width):
-                channel(i * width + slot)
+                channel(i * width + slot, tips)
             return carry
 
         lax.fori_loop(first // width, last // width, group, 0)
@@ -170,25 +172,19 @@
     pair_lists(steps, regions, region, order_ref, channels_ref, list_ref)
     load.wait()
 
+    def place(at, row, value):
+        ext[at, row : row + value.shape[1]] = value
+        turned[at, row : row + value.shape[1]] = pltpu.roll(value, 64, 2)
+
     def lay_out(i, carry):
         at = pl.ds(pl.multiple_of(i * 16, 16), 16)
-        ext[at, 0:blocks] = local[at, :].astype(jnp.float32).reshape(16, blocks, 128)
+        place(at, 0, local[at, :].astype(jnp.float32).reshape(16, blocks, 128))
         return carry
 
     lax.fori_loop(0, chans // 16, lay_out, 0)
     rest = chans // 16 * 16
     if rest < chans:
-        ext[rest:chans, 0:blocks] = local[rest:chans, :].astype(jnp.float32).reshape(chans - rest, blocks, 128)
-    edge_copy.wait()
-    inside = (me < count - 1) & (lax.broadcasted_iota(jnp.int32, (1, depth), 1) < taps - 1)
-    for i in range(0, chans, 16):
-        end = min(i + 16, chans)
-        rim = jnp.where(inside, halo[i:end].astype(jnp.float32), 0.0)
-        ext[i:end, blocks : blocks + 2] = rim.reshape(end - i, 2, 128)
-    early = chans // 4 // width * width
-    late = chans * 3 // 4 // width * width
-    windows(0, early)
-
+        place(pl.ds(rest, chans - rest), 0, local[rest:chans, :].astype(jnp.float32).reshape(chans - rest, blocks, 128))
     for u in range(tiles):
         @pl.when(me != holders[u])
         def _():
@@ -218,7 +214,18 @@
             spread_copy(e).start()
         spread_copy(0).start()
 
-    windows(early, late)
+    edge_copy.wait()
+    inside = (me < count - 1) & (lax.broadcasted_iota(jnp.int32, (1, depth), 1) < taps - 1)
+    rims = []
+    for i in range(0, chans, 16):
+        end = min(i + 16, chans)
+        rim = jnp.where(inside, halo[i:end].astype(jnp.float32), 0.0)
+        rims.append(rim[:, 128:])
+        place(pl.ds(i, end - i), blocks, rim.reshape(end - i, 2, 128))
+    tips = jnp.concatenate(rims + [jnp.zeros((128 - chans, 128), jnp.float32)], axis=0).T
+    tips = [tips[0:8], tips[64:72]]
+    late = chans * 5 // 6 // width * width
+    windows(0, late, tips)
 
     def pass_copy(v):
         u = 2 * v + core
@@ -233,7 +240,7 @@
             pass_copy(v).wait_recv()
             pass_copy(v).start()
 
-    windows(late, chans)
+    windows(late, chans, tips)
 
     for v in range(half):
         u = 2 * v + 1 - core
@@ -366,6 +373,7 @@
             pltpu.VMEM((chans, depth), jnp.bfloat16),
             pltpu.VMEM((chans, time_local), jnp.bfloat16),
             pltpu.VMEM((chans, blocks + 8, 128), jnp.float32),
+            pltpu.VMEM((chans, blocks + 8, 128), jnp.float32),
             dma,
             dma((2,)),
             dma((tiles,)),
@@ -374,7 +382,7 @@
             dma((tiles,)),
             dma((tiles // 2,)),
         ],
-        compiler_params=pltpu.CompilerParams(collective_id=0, has_side_effects=True, vmem_limit_bytes=16 * 2**20),
+        compiler_params=pltpu.CompilerParams(collective_id=0, has_side_effects=True, vmem_limit_bytes=28 * 2**20),
         name="prepare",
     )(*[pltpu.with_memory_space_constraint(v, pltpu.HBM) for v in (
         owner, library.reshape(templates * used, tap_count), waveform,

time: 42.2 us -> 40.2 us (0.953)
  Pallas kernels: 36.2 us -> 34.5 us
  waiting for transfers between devices: 3.27 us -> 2.52 us
    pallas_call x1, Pallas kernels: 20.4 us -> 17.6 us  [body(): pl.pallas_call(functools.partial(prepare_kernel, steps, count, regions),...]
    pallas_call x1, Pallas kernels: 7 us -> 8.18 us  [body(): pl.pallas_call(functools.partial(finish_kernel, time_local * count, count...]
    ppermute x1, waiting for transfers between devices: 3.27 us -> 2.52 us  [body(): lax.ppermute(part, 'region', [(i, (i + d) % regions) for i in range(regio...]
  transfers between devices with their start and end apart: 1 -> 1, of which waited for: 1 -> 1; matrix products, arithmetic and copies ran while one was open for 0% -> 0% of each run, Pallas kernels for 10% -> 11%
where the time goes in v4:
time: 40.2 us; the launch traced here: 39.6 us
  Pallas kernels  34.5 us (86%)
  waiting for transfers between devices  2.52 us (6%)
  starting transfers between devices  1.56 us (4%)
  local copies, waits for them, and re-layouts  1.01 us (3%)
    pallas_call x1, Pallas kernels, body(): pl.pallas_call(functools.partial(prepare_kernel, steps, count, regions),...  17.6 us
    pallas_call x2, Pallas kernels, partial_sums(): pl.pallas_call(functools.partial(pair_kernel, which), out_shape=jax.Shape...  8.75 us
    pallas_call x1, Pallas kernels, body(): pl.pallas_call(functools.partial(finish_kernel, time_local * count, count...  8.18 us
    ppermute x1, waiting for transfers between devices, body(): lax.ppermute(part, 'region', [(i, (i + d) % regions) for i in range(regio...  2.52 us
    ppermute x1, starting transfers between devices, body(): lax.ppermute(part, 'region', [(i, (i + d) % regions) for i in range(regio...  1.56 us
    reshape x1, local copies, waits for them, and re-layouts, body(): return result.reshape(steps, per, time_local)  1.01 us
  transfers between devices with their start and end apart: 1, of which 1 were waited for; matrix products, arithmetic and copies ran while one was open for 0% of the time, Pallas kernels for 11%

profile of v4, /device:TPU:0, one launch (start us, length us, event | category | flops | bytes accessed | tf_op | source)
XLA Modules:
  0.0 39.6 jit_solution(7541974085404397501)
XLA Ops:
  0.0 17.6 %prepare.1 = (bf16[96,288,128]{2,1,0:T(8,128)(2,1)S(1)}, f32[96,32,256]{2,1,0:T(8,128)S(1)}, f32[776,256]{1,0:T(8,128)S(1)}, s32[2,1,640]{2,1,0:T(1,128)S(1)}) custom-call(s32[4]{0:T(128)} %owner_hbm.1, f32[192,200]{1,0:T(8,128)} %bitcast.3, bf16[96,8192]{1,0:T(8,128)(2,1)} %x_ref.1, s32[1,96]{1,0:T(1,128)} %bitcast.5, s32[32,24]{1,0:T(8,128)} %bitcast.4), custom_call_target="tpu_custom_call" | custom-call | tf_op jit(solution)/shard_map/prepare/pallas_call | solution.py:353
  17.6 4.4 %pairs.2 = bf16[16,32,256]{2,1,0:T(8,128)(2,1)S(1)} custom-call(s32[2,1,640]{2,1,0:T(1,128)S(1)} %get-tuple-element.9.list_ref, bf16[96,288,128]{2,1,0:T(8,128)(2,1)S(1)} %get-tuple-element.10.z_ref, f32[96,32,256]{2,1,0:T(8,128)S(1)} %get-tuple-element.11.inv_ref, f32[776,256]{1,0:T(8,128)S(1)} %get-tuple-element.12.taps_ref), custom_call_target="tpu_custom_call" | custom-call | flops 805306368 | bytes 12582912 | tf_op jit(solution)/shard_map/pairs/pallas_call | solution.py:393
  22.0 1.6 %collective-permute-start = (bf16[16,32,256]{2,1,0:T(8,128)(2,1)S(1)}, bf16[16,32,256]{2,1,0:T(8,128)(2,1)S(1)}, u32[]{:S(2)}, u32[]{:S(2)}) collective-permute-start(bf16[16,32,256]{2,1,0:T(8,128)(2,1)S(1)} %pairs.2), channel_id=1, source_target_pairs={{0,1},{1,0},{2,3},{3,2},{4,5},{5,4},{6,7},{7,6},{8,9},{9,8},{10,11... | collective-permute-start | bytes 786440 | tf_op jit(solution)/shard_map/ppermute | solution.py:407
  23.5 4.4 %pairs.3.refs_1_ = f32[16,32,256]{2,1,0:T(8,128)S(1)} custom-call(s32[2,1,640]{2,1,0:T(1,128)S(1)} %get-tuple-element.9.list_ref, bf16[96,288,128]{2,1,0:T(8,128)(2,1)S(1)} %get-tuple-element.10.z_ref, f32[96,32,256]{2,1,0:T(8,128)S(1)} %get-tuple-element.11.inv_ref, f32[776,256]{1,0:T(8,128)S(1)} %get-tuple-element.12.taps_ref), custom_call_target="tpu_custom_call" | custom-call | flops 805306368 | bytes 12582912 | tf_op jit(solution)/shard_map/pairs/pallas_call | solution.py:393
  27.9 2.5 %collective-permute-done.refs_0_ = bf16[16,32,256]{2,1,0:T(8,128)(2,1)S(1)} collective-permute-done((bf16[16,32,256]{2,1,0:T(8,128)(2,1)S(1)}, bf16[16,32,256]{2,1,0:T(8,128)(2,1)S(1)}, u32[]{:S(2)}, u32[]{:S(2)}) %collective-permute-start) | collective-permute-done | bytes 262176 | tf_op jit(solution)/shard_map/ppermute | solution.py:407
  30.4 8.2 %finish.1 = f32[16,64,128]{2,1,0:T(8,128)S(1)} custom-call(bf16[16,32,256]{2,1,0:T(8,128)(2,1)S(1)} %collective-permute-done.refs_0_, f32[16,32,256]{2,1,0:T(8,128)S(1)} %pairs.3.refs_1_), custom_call_target="tpu_custom_call" | custom-call | tf_op jit(solution)/shard_map/finish/pallas_call | solution.py:410
  38.6 1.0 %reshape.15 = f32[4,4,8192]{2,1,0:T(4,128)} reshape(f32[16,64,128]{2,1,0:T(8,128)S(1)} %finish.1) | data formatting | bytes 1048576 | tf_op jit(solution)/shard_map/reshape | solution.py:425
Async XLA Ops:
  22.0 8.5 %collective-permute-start = (bf16[16,32,256]{2,1,0:T(8,128)(2,1)S(1)}, bf16[16,32,256]{2,1,0:T(8,128)(2,1)S(1)}, u32[]{:S(2)}, u32[]{:S(2)}) collective-permute-start(bf16[16,32,256]{2,1,0:T(8,128)(2,1)S(1)} %pairs.2), channel_id=1, source_target_pairs={{0,1},{1,0},{2,3},{3,2},{4,5},{5,4},{6,7},{7,6},{8,9},{9,8},{10,11... | collective-permute-start | bytes 786440 | tf_op jit(solution)/shard_map/ppermute | solution.py:407

commit v5 on v4

--- a/solution.py
+++ b/solution.py
@@ -11,7 +11,7 @@
 offs = 32
 depth = 256
 rows_z = 288
-unroll = 32
+unroll = 64
 MESH = pl.DeviceIdType.MESH
 
 
@@ -118,7 +118,6 @@
         src_ref=x_ref.at[:, pl.ds(0, depth)], dst_ref=halo, send_sem=halo_sems.at[0], recv_sem=halo_sems.at[1],
         device_id=(left, region), device_id_type=MESH,
     )
-    edge_copy.start()
 
     def piece(u):
         return pltpu.make_async_remote_copy(
@@ -130,6 +129,10 @@
         @pl.when(me != holders[u])
         def _():
             piece(u).start()
+
+    @pl.when(me > 0)
+    def _():
+        edge_copy.start()
 
     chans = x_ref.shape[0]
     blocks = x_ref.shape[1] // 128
@@ -214,7 +217,10 @@
             spread_copy(e).start()
         spread_copy(0).start()
 
-    edge_copy.wait()
+    @pl.when(me < count - 1)
+    def _():
+        edge_copy.wait_recv()
+
     inside = (me < count - 1) & (lax.broadcasted_iota(jnp.int32, (1, depth), 1) < taps - 1)
     rims = []
     for i in range(0, chans, 16):
@@ -252,6 +258,10 @@
     taps_ref[0 : tiles * steps * 16] = full[...].astype(jnp.float32).reshape(tiles * steps * 16, depth)
     taps_ref[tiles * steps * 16 :] = jnp.zeros((8, depth), jnp.float32)
 
+    @pl.when(me > 0)
+    def _():
+        edge_copy.wait_send()
+
     @pl.when(holding)
     def _():
         for e in range(chips):
@@ -263,8 +273,9 @@
             pass_copy(v).wait_send()
 
 
-def pair_kernel(which, list_ref, z_ref, inv_ref, taps_ref, out_ref, acc_ref):
+def pair_kernel(which, first, list_ref, z_ref, inv_ref, taps_ref, out_ref, acc_ref):
     held = out_ref.shape[0]
+    tiles = out_ref.shape[2] // 128
     total = list_ref[which, 0, list_ref.shape[2] - 1]
     acc_ref[...] = jnp.zeros_like(acc_ref)
 
@@ -276,9 +287,9 @@
         codes = [list_ref[which, 0, 2 * e + i] for i in range(2)]
         matrix = jnp.concatenate([shifted(codes[i] & 1023) for i in range(2)], axis=0).astype(jnp.bfloat16)
         col = (codes[0] >> 10) & 127
-        window = jnp.concatenate([z_ref[col, 0:depth], z_ref[col, offs : offs + depth]], axis=1)
+        window = jnp.concatenate([z_ref[col, offs * v : offs * v + depth] for v in range(first, first + tiles)], axis=1)
         product = jnp.dot(matrix, window, preferred_element_type=jnp.float32)
-        scale = inv_ref[col]
+        scale = inv_ref[col, :, first * 128 : (first + tiles) * 128]
         return [(codes[i] >> 17, product[i * offs : (i + 1) * offs] * scale) for i in range(2)]
 
     def group(i, carry):
@@ -304,8 +315,8 @@
     power = jnp.zeros((1, 128), jnp.float32)
     for at in range(held):
         value = parts[-1][at]
-        for other in parts[:-1]:
-            value = value + other[at].astype(jnp.float32)
+        for i in range(0, len(parts) - 1, 2):
+            value = value + jnp.concatenate([parts[i][at], parts[i + 1][at]], axis=1).astype(jnp.float32)
         stacked[at] = value
         total = jnp.sum(jnp.sum(value * value, axis=0, keepdims=True), axis=1, keepdims=True)
         power = power + jnp.where(lane == at, total, 0.0)
@@ -389,9 +400,9 @@
         station_order.reshape(1, chans), channels.reshape(all_templates, used),
     )])
 
-    def partial_sums(which, dtype):
+    def partial_sums(which, dtype, first, lanes):
         return pl.pallas_call(
-            functools.partial(pair_kernel, which),
+            functools.partial(pair_kernel, which, first),
             out_shape=jax.ShapeDtypeStruct((held, offs, lanes), dtype),
             in_specs=[smem, vmem, vmem, vmem],
             out_specs=vmem,
@@ -403,14 +414,15 @@
 
     parts = []
     for d in range(1, regions):
-        part = partial_sums(d - 1, jnp.bfloat16)
-        parts.append(lax.ppermute(part, "region", [(i, (i + d) % regions) for i in range(regions)]))
-    parts.append(partial_sums(regions - 1, jnp.float32))
+        for v in range(lanes // 128):
+            part = partial_sums(d - 1, jnp.bfloat16, v, 128)
+            parts.append(lax.ppermute(part, "region", [(i, (i + d) % regions) for i in range(regions)]))
+    parts.append(partial_sums(regions - 1, jnp.float32, 0, lanes))
 
     result = pl.pallas_call(
         functools.partial(finish_kernel, time_local * count, count),
         out_shape=jax.ShapeDtypeStruct((held, blocks, 128), jnp.float32),
-        in_specs=[vmem] * regions,
+        in_specs=[vmem] * len(parts),
         out_specs=vmem,
         scratch_shapes=[
             pltpu.VMEM((held, offs, lanes), jnp.float32),

time: 40.2 us -> 38.7 us (0.963)
  waiting for transfers between devices: 2.52 us -> 0.78 us
  starting transfers between devices: 1.56 us -> 2.16 us
    ppermute x1 -> x2, waiting for transfers between devices: 2.52 us -> 0.78 us  [body(): lax.ppermute(part, 'region', [(i, (i + d) % regions) for i in range(regio...]
    ppermute x1 -> x2, starting transfers between devices: 1.56 us -> 2.16 us  [body(): lax.ppermute(part, 'region', [(i, (i + d) % regions) for i in range(regio...]
    pallas_call x2 -> x3, Pallas kernels: 8.75 us -> 9.34 us  [partial_sums(): pl.pallas_call(functools.partial(pair_kernel, which, first), out_shape=ja...]
  transfers between devices with their start and end apart: 1 -> 2, of which waited for: 1 -> 1; matrix products, arithmetic and copies ran while one was open for 0% -> 0% of each run, Pallas kernels for 11% -> 17%
where the time goes in v5:
time: 38.7 us; the launch traced here: 38.5 us
  Pallas kernels  34.5 us (89%)
  starting transfers between devices  2.16 us (6%)
  local copies, waits for them, and re-layouts  1.01 us (3%)
  waiting for transfers between devices  0.78 us (2%)
    pallas_call x1, Pallas kernels, body(): pl.pallas_call(functools.partial(prepare_kernel, steps, count, regions),...  17.2 us
    pallas_call x3, Pallas kernels, partial_sums(): pl.pallas_call(functools.partial(pair_kernel, which, first), out_shape=ja...  9.34 us
    pallas_call x1, Pallas kernels, body(): pl.pallas_call(functools.partial(finish_kernel, time_local * count, count...  7.99 us
    ppermute x2, starting transfers between devices, body(): lax.ppermute(part, 'region', [(i, (i + d) % regions) for i in range(regio...  2.16 us
    reshape x1, local copies, waits for them, and re-layouts, body(): return result.reshape(steps, per, time_local)  1.01 us
    ppermute x2, waiting for transfers between devices, body(): lax.ppermute(part, 'region', [(i, (i + d) % regions) for i in range(regio...  0.78 us
  transfers between devices with their start and end apart: 2, of which 1 were waited for; matrix products, arithmetic and copies ran while one was open for 0% of the time, Pallas kernels for 17%

profile of v5, /device:TPU:0, one launch (start us, length us, event | category | flops | bytes accessed | tf_op | source)
XLA Modules:
  0.0 38.5 jit_solution(4551419748438855696)
XLA Ops:
  0.0 17.2 %prepare.1 = (bf16[96,288,128]{2,1,0:T(8,128)(2,1)S(1)}, f32[96,32,256]{2,1,0:T(8,128)S(1)}, f32[776,256]{1,0:T(8,128)S(1)}, s32[2,1,640]{2,1,0:T(1,128)S(1)}) custom-call(s32[4]{0:T(128)} %owner_hbm.1, f32[192,200]{1,0:T(8,128)} %bitcast.3, bf16[96,8192]{1,0:T(8,128)(2,1)} %x_ref.1, s32[1,96]{1,0:T(1,128)} %bitcast.5, s32[32,24]{1,0:T(8,128)} %bitcast.4), custom_call_target="tpu_custom_call" | custom-call | tf_op jit(solution)/shard_map/prepare/pallas_call | solution.py:364
  17.2 2.7 %pairs.3 = bf16[16,32,128]{2,1,0:T(8,128)(2,1)S(1)} custom-call(s32[2,1,640]{2,1,0:T(1,128)S(1)} %get-tuple-element.9.list_ref, bf16[96,288,128]{2,1,0:T(8,128)(2,1)S(1)} %get-tuple-element.10.z_ref, f32[96,32,256]{2,1,0:T(8,128)S(1)} %get-tuple-element.11.inv_ref, f32[776,256]{1,0:T(8,128)S(1)} %get-tuple-element.12.taps_ref), custom_call_target="tpu_custom_call" | custom-call | flops 402653184 | bytes 12582912 | tf_op jit(solution)/shard_map/pairs/pallas_call | solution.py:404
  19.9 1.6 %collective-permute-start = (bf16[16,32,128]{2,1,0:T(8,128)(2,1)S(1)}, bf16[16,32,128]{2,1,0:T(8,128)(2,1)S(1)}, u32[]{:S(2)}, u32[]{:S(2)}) collective-permute-start(bf16[16,32,128]{2,1,0:T(8,128)(2,1)S(1)} %pairs.3), channel_id=1, source_target_pairs={{0,1},{1,0},{2,3},{3,2},{4,5},{5,4},{6,7},{7,6},{8,9},{9,8},{10,11... | collective-permute-start | bytes 393224 | tf_op jit(solution)/shard_map/ppermute | solution.py:419
  21.5 2.7 %pairs.4 = bf16[16,32,128]{2,1,0:T(8,128)(2,1)S(1)} custom-call(s32[2,1,640]{2,1,0:T(1,128)S(1)} %get-tuple-element.9.list_ref, bf16[96,288,128]{2,1,0:T(8,128)(2,1)S(1)} %get-tuple-element.10.z_ref, f32[96,32,256]{2,1,0:T(8,128)S(1)} %get-tuple-element.11.inv_ref, f32[776,256]{1,0:T(8,128)S(1)} %get-tuple-element.12.taps_ref), custom_call_target="tpu_custom_call" | custom-call | flops 402653184 | bytes 12582912 | tf_op jit(solution)/shard_map/pairs/pallas_call | solution.py:404
  24.1 0.6 %collective-permute-start.1 = (bf16[16,32,128]{2,1,0:T(8,128)(2,1)S(1)}, bf16[16,32,128]{2,1,0:T(8,128)(2,1)S(1)}, u32[]{:S(2)}, u32[]{:S(2)}) collective-permute-start(bf16[16,32,128]{2,1,0:T(8,128)(2,1)S(1)} %pairs.4), channel_id=1, source_target_pairs={{0,1},{1,0},{2,3},{3,2},{4,5},{5,4},{6,7},{7,6},{8,9},{9,8},{10,11... | collective-permute-start | bytes 393224 | tf_op jit(solution)/shard_map/ppermute | solution.py:419
  24.7 4.0 %pairs.5.refs_2_ = f32[16,32,256]{2,1,0:T(8,128)S(1)} custom-call(s32[2,1,640]{2,1,0:T(1,128)S(1)} %get-tuple-element.9.list_ref, bf16[96,288,128]{2,1,0:T(8,128)(2,1)S(1)} %get-tuple-element.10.z_ref, f32[96,32,256]{2,1,0:T(8,128)S(1)} %get-tuple-element.11.inv_ref, f32[776,256]{1,0:T(8,128)S(1)} %get-tuple-element.12.taps_ref), custom_call_target="tpu_custom_call" | custom-call | flops 805306368 | bytes 12582912 | tf_op jit(solution)/shard_map/pairs/pallas_call | solution.py:404
  28.7 0.0 collective-permute-done.refs_0_
  28.8 0.8 %collective-permute-done.1.refs_1_ = bf16[16,32,128]{2,1,0:T(8,128)(2,1)S(1)} collective-permute-done((bf16[16,32,128]{2,1,0:T(8,128)(2,1)S(1)}, bf16[16,32,128]{2,1,0:T(8,128)(2,1)S(1)}, u32[]{:S(2)}, u32[]{:S(2)}) %collective-permute-start.1) | collective-permute-done | bytes 131104 | tf_op jit(solution)/shard_map/ppermute | solution.py:419
  29.5 8.0 %finish.1 = f32[16,64,128]{2,1,0:T(8,128)S(1)} custom-call(bf16[16,32,128]{2,1,0:T(8,128)(2,1)S(1)} %collective-permute-done.refs_0_, bf16[16,32,128]{2,1,0:T(8,128)(2,1)S(1)} %collective-permute-done.1.refs_1_, f32[16,32,256]{2,1,0:T(8,128)S(1)} %pairs.5.refs_2_), custom_call_target="tpu_custom_call" | custom-call | tf_op jit(solution)/shard_map/finish/pallas_call | solution.py:422
  37.5 1.0 %reshape.15 = f32[4,4,8192]{2,1,0:T(4,128)} reshape(f32[16,64,128]{2,1,0:T(8,128)S(1)} %finish.1) | data formatting | bytes 1048576 | tf_op jit(solution)/shard_map/reshape | solution.py:437
Async XLA Ops:
  19.9 8.9 %collective-permute-start = (bf16[16,32,128]{2,1,0:T(8,128)(2,1)S(1)}, bf16[16,32,128]{2,1,0:T(8,128)(2,1)S(1)}, u32[]{:S(2)}, u32[]{:S(2)}) collective-permute-start(bf16[16,32,128]{2,1,0:T(8,128)(2,1)S(1)} %pairs.3), channel_id=1, source_target_pairs={{0,1},{1,0},{2,3},{3,2},{4,5},{5,4},{6,7},{7,6},{8,9},{9,8},{10,11... | collective-permute-start | bytes 393224 | tf_op jit(solution)/shard_map/ppermute | solution.py:419
  24.1 5.4 %collective-permute-start.1 = (bf16[16,32,128]{2,1,0:T(8,128)(2,1)S(1)}, bf16[16,32,128]{2,1,0:T(8,128)(2,1)S(1)}, u32[]{:S(2)}, u32[]{:S(2)}) collective-permute-start(bf16[16,32,128]{2,1,0:T(8,128)(2,1)S(1)} %pairs.4), channel_id=1, source_target_pairs={{0,1},{1,0},{2,3},{3,2},{4,5},{5,4},{6,7},{7,6},{8,9},{9,8},{10,11... | collective-permute-start | bytes 393224 | tf_op jit(solution)/shard_map/ppermute | solution.py:419

commit v6 on v5

--- a/solution.py
+++ b/solution.py
@@ -13,6 +13,10 @@
 rows_z = 288
 unroll = 64
 MESH = pl.DeviceIdType.MESH
+
+
+def far_first(count):
+    return sorted(range(1, count), key=lambda d: abs(d - count // 2))
 
 
 def pair_lists(steps, regions, region, order_ref, channels_ref, list_ref):
@@ -78,7 +82,7 @@
     me = lax.axis_index("tm")
     region = lax.axis_index("region")
     barrier = pltpu.get_barrier_semaphore()
-    for d in range(1, count):
+    for d in far_first(count):
         pl.semaphore_signal(barrier, inc=1, device_id=(lax.rem(me + d, count), region), device_id_type=MESH)
     small = [
         pltpu.make_async_copy(source, target, small_sems.at[i])
@@ -90,27 +94,27 @@
         copy.start()
     load = pltpu.make_async_copy(x_ref, local, local_sem)
     load.start()
-    for copy in small:
-        copy.wait()
+    small[0].wait()
 
     taps = library_ref.shape[1]
-    tiles = mine.shape[0]
+    units = mine.shape[0]
+    seats = full.shape[0]
+    share = units // seats
     panel = library_ref[...]
-    centred = panel - jnp.sum(panel, axis=1, keepdims=True) / taps
-    normed = centred / jnp.sqrt(jnp.sum(centred * centred, axis=1, keepdims=True) + eps)
+    centred = panel - jnp.sum(panel, axis=1, keepdims=True) * (1 / taps)
+    normed = centred * lax.rsqrt(jnp.sum(centred * centred, axis=1, keepdims=True) + eps)
     normed = jnp.concatenate([normed, jnp.zeros((panel.shape[0], depth - taps), jnp.float32)], axis=1)
-    mine[...] = normed.astype(jnp.bfloat16).reshape(tiles, 16, depth)
-
-    half = tiles // 2
+    normed = normed.astype(jnp.bfloat16)
+    for i in range(units):
+        mine[i] = normed[i // 2 * 16 : i // 2 * 16 + 16, i % 2 * 128 : i % 2 * 128 + 128]
+
+    first = (count - seats) // 4 * 2
     chips = count // 2
     chip = me // 2
     core = me % 2
     sibling = chip * 2 + 1 - core
-    seats = [v * chips // half for v in range(half)]
-    holders = [seats[u // 2] * 2 + u % 2 for u in range(tiles)]
-    seat = (chip * half + chips - 1) // chips
-    holding = seat * chips // half == chip
-    my_tile = jnp.minimum(seat, half - 1) * 2 + core
+    holding = (me >= first) & (me < first + seats)
+    seat = jnp.clip(me - first, 0, seats - 1)
 
     pl.semaphore_wait(barrier, count - 1)
     left = lax.rem(me + count - 1, count)
@@ -121,12 +125,13 @@
 
     def piece(u):
         return pltpu.make_async_remote_copy(
-            src_ref=mine.at[u], dst_ref=got.at[me], send_sem=one_send.at[u], recv_sem=one_recv.at[me],
-            device_id=(holders[u], region), device_id_type=MESH,
+            src_ref=mine.at[pl.ds(u * share, share)], dst_ref=got.at[me],
+            send_sem=one_send.at[u], recv_sem=one_recv.at[me],
+            device_id=(first + u, region), device_id_type=MESH,
         )
 
-    for u in range(tiles):
-        @pl.when(me != holders[u])
+    for u in range(seats):
+        @pl.when(me != first + u)
         def _():
             piece(u).start()
 
@@ -172,6 +177,8 @@
 
         lax.fori_loop(first // width, last // width, group, 0)
 
+    for copy in small[1:]:
+        copy.wait()
     pair_lists(steps, regions, region, order_ref, channels_ref, list_ref)
     load.wait()
 
@@ -188,15 +195,10 @@
     rest = chans // 16 * 16
     if rest < chans:
         place(pl.ds(rest, chans - rest), 0, local[rest:chans, :].astype(jnp.float32).reshape(chans - rest, blocks, 128))
-    for u in range(tiles):
-        @pl.when(me != holders[u])
-        def _():
-            piece(u).wait_send()
-
     def spread_copy(e):
         peer = sibling if e == 0 else lax.rem(chip + e, chips) * 2 + core
         return pltpu.make_async_remote_copy(
-            src_ref=sel, dst_ref=full.at[my_tile], send_sem=two_send.at[e], recv_sem=two_recv.at[my_tile],
+            src_ref=sel, dst_ref=full.at[seat], send_sem=two_send.at[e], recv_sem=two_recv.at[seat],
             device_id=(peer, region), device_id_type=MESH,
         )
 
@@ -206,14 +208,14 @@
             @pl.when(me != i)
             def _():
                 pltpu.make_async_remote_copy(
-                    src_ref=mine.at[0], dst_ref=got.at[i], send_sem=one_send.at[0], recv_sem=one_recv.at[i],
+                    src_ref=mine.at[pl.ds(0, share)], dst_ref=got.at[i], send_sem=one_send.at[0], recv_sem=one_recv.at[i],
                     device_id=(left, region), device_id_type=MESH,
                 ).wait_recv()
-        got[me] = mine[my_tile]
+        got[me] = mine[pl.ds(seat * share, share)]
         for s in range(steps):
             sel[s] = got[owner_ref[s]]
-        full[my_tile] = sel[...]
-        for e in range(1, chips):
+        full[seat] = sel[...]
+        for e in far_first(chips):
             spread_copy(e).start()
         spread_copy(0).start()
 
@@ -240,35 +242,43 @@
             device_id=(sibling, region), device_id_type=MESH,
         )
 
-    for v in range(half):
-        @pl.when(chip != seats[v])
+    for v in range(seats // 2):
+        @pl.when(chip != first // 2 + v)
         def _():
             pass_copy(v).wait_recv()
             pass_copy(v).start()
 
     windows(late, chans, tips)
 
-    for v in range(half):
+    for v in range(seats // 2):
         u = 2 * v + 1 - core
         pltpu.make_async_remote_copy(
             src_ref=sel, dst_ref=full.at[u], send_sem=two_send.at[0], recv_sem=two_recv.at[u],
             device_id=(sibling, region), device_id_type=MESH,
         ).wait_recv()
 
-    taps_ref[0 : tiles * steps * 16] = full[...].astype(jnp.float32).reshape(tiles * steps * 16, depth)
-    taps_ref[tiles * steps * 16 :] = jnp.zeros((8, depth), jnp.float32)
+    span = steps * 16
+    for i in range(units):
+        value = full[i // share, :, i % share].astype(jnp.float32).reshape(span, 128)
+        taps_ref[i // 2 * span : i // 2 * span + span, i % 2 * 128 : i % 2 * 128 + 128] = value
+    taps_ref[units // 2 * span :] = jnp.zeros((8, depth), jnp.float32)
 
     @pl.when(me > 0)
     def _():
         edge_copy.wait_send()
+
+    for u in range(seats):
+        @pl.when(me != first + u)
+        def _():
+            piece(u).wait_send()
 
     @pl.when(holding)
     def _():
         for e in range(chips):
             spread_copy(e).wait_send()
 
-    for v in range(half):
-        @pl.when(chip != seats[v])
+    for v in range(seats // 2):
+        @pl.when(chip != first // 2 + v)
         def _():
             pass_copy(v).wait_send()
 
@@ -308,22 +318,25 @@
     me = lax.axis_index("tm")
     region = lax.axis_index("region")
     barrier = pltpu.get_barrier_semaphore()
-    for d in range(1, count):
+    for d in far_first(count):
         pl.semaphore_signal(barrier, inc=1, device_id=(lax.rem(me + d, count), region), device_id_type=MESH)
     held = out_ref.shape[0]
-    lane = lax.broadcasted_iota(jnp.int32, (1, 128), 1)
-    power = jnp.zeros((1, 128), jnp.float32)
+    squares = []
     for at in range(held):
         value = parts[-1][at]
         for i in range(0, len(parts) - 1, 2):
             value = value + jnp.concatenate([parts[i][at], parts[i + 1][at]], axis=1).astype(jnp.float32)
         stacked[at] = value
-        total = jnp.sum(jnp.sum(value * value, axis=0, keepdims=True), axis=1, keepdims=True)
-        power = power + jnp.where(lane == at, total, 0.0)
+        square = value * value
+        square = square[:, :128] + square[:, 128:]
+        squares.append(jnp.sum(square.reshape(offs // 8, 8, 128), axis=0)[None])
+    power = jnp.sum(jnp.sum(jnp.concatenate(squares, axis=0), axis=1), axis=1, keepdims=True)
+    diagonal = lax.broadcasted_iota(jnp.int32, (held, 128), 0) == lax.broadcasted_iota(jnp.int32, (held, 128), 1)
+    power = jnp.sum(jnp.where(diagonal, power, 0.0), axis=0, keepdims=True)
     power_sent[...] = power
     pl.semaphore_wait(barrier, count - 1)
     copies = []
-    for d in range(1, count):
+    for d in far_first(count):
         copy = pltpu.make_async_remote_copy(
             src_ref=power_sent, dst_ref=power_got.at[d - 1], send_sem=p_send.at[d - 1], recv_sem=p_recv.at[d - 1],
             device_id=(lax.rem(me + d, count), region), device_id_type=MESH,
@@ -335,12 +348,14 @@
         turned = jnp.concatenate([value[:, :128], value[:, 128:]], axis=0).T
         out_ref[at] = jnp.concatenate([turned[:64], turned[64:]], axis=1)
     for copy in copies:
-        copy.wait()
+        copy.wait_recv()
     power = power + jnp.sum(power_got[...], axis=0)
     factor = lax.rsqrt(power / total_time + eps)
+    scale = jnp.sum(jnp.where(diagonal, factor, 0.0), axis=1, keepdims=True)
     for at in range(held):
-        one = jnp.sum(jnp.where(lane == at, factor, 0.0), axis=1, keepdims=True)
-        out_ref[at] = out_ref[at] * one
+        out_ref[at] = out_ref[at] * scale[at : at + 1]
+    for copy in copies:
+        copy.wait_send()
 
 
 def body(waveform, station_order, library, owner, channels):
@@ -354,7 +369,8 @@
     held = steps * per
     all_templates = steps * templates
     pairs = all_templates * used
-    tiles = templates * used // 16
+    units = templates * used // 8
+    seats = 8
     lanes = time_local // offs
 
     vmem = pl.BlockSpec(memory_space=pltpu.VMEM)
@@ -377,21 +393,21 @@
             pltpu.VMEM((1, chans), jnp.int32),
             pltpu.VMEM((all_templates, used), jnp.int32),
             dma((4,)),
-            pltpu.VMEM((tiles, 16, depth), jnp.bfloat16),
-            pltpu.VMEM((count, 16, depth), jnp.bfloat16),
-            pltpu.VMEM((steps, 16, depth), jnp.bfloat16),
-            pltpu.VMEM((tiles, steps, 16, depth), jnp.bfloat16),
+            pltpu.VMEM((units, 16, 128), jnp.bfloat16),
+            pltpu.VMEM((count, units // seats, 16, 128), jnp.bfloat16),
+            pltpu.VMEM((steps, units // seats, 16, 128), jnp.bfloat16),
+            pltpu.VMEM((seats, steps, units // seats, 16, 128), jnp.bfloat16),
             pltpu.VMEM((chans, depth), jnp.bfloat16),
             pltpu.VMEM((chans, time_local), jnp.bfloat16),
             pltpu.VMEM((chans, blocks + 8, 128), jnp.float32),
             pltpu.VMEM((chans, blocks + 8, 128), jnp.float32),
             dma,
             dma((2,)),
-            dma((tiles,)),
+            dma((seats,)),
             dma((count,)),
             dma((count // 2,)),
-            dma((tiles,)),
-            dma((tiles // 2,)),
+            dma((seats,)),
+            dma((seats // 2,)),
         ],
         compiler_params=pltpu.CompilerParams(collective_id=0, has_side_effects=True, vmem_limit_bytes=28 * 2**20),
         name="prepare",

time: 38.7 us -> 38.5 us (level)
    pallas_call x1, Pallas kernels: 7.99 us -> 7.05 us  [body(): pl.pallas_call(functools.partial(finish_kernel, time_local * count, count...]
    pallas_call x1, Pallas kernels: 17.2 us -> 18.1 us  [body(): pl.pallas_call(functools.partial(prepare_kernel, steps, count, regions),...]
where the time goes in v6:
time: 38.5 us; the launch traced here: 38.4 us
  Pallas kernels  34.5 us (90%)
  starting transfers between devices  2.15 us (6%)
  local copies, waits for them, and re-layouts  1.01 us (3%)
  waiting for transfers between devices  0.64 us (2%)
    pallas_call x1, Pallas kernels, body(): pl.pallas_call(functools.partial(prepare_kernel, steps, count, regions),...  18.1 us
    pallas_call x3, Pallas kernels, partial_sums(): pl.pallas_call(functools.partial(pair_kernel, which, first), out_shape=ja...  9.38 us
    pallas_call x1, Pallas kernels, body(): pl.pallas_call(functools.partial(finish_kernel, time_local * count, count...  7.05 us
    ppermute x2, starting transfers between devices, body(): lax.ppermute(part, 'region', [(i, (i + d) % regions) for i in range(regio...  2.15 us
    reshape x1, local copies, waits for them, and re-layouts, body(): return result.reshape(steps, per, time_local)  1.01 us
  transfers between devices with their start and end apart: 2, of which 1 were waited for; matrix products, arithmetic and copies ran while one was open for 0% of the time, Pallas kernels for 17%

profile of v6, /device:TPU:0, one launch (start us, length us, event | category | flops | bytes accessed | tf_op | source)
XLA Modules:
  0.0 38.4 jit_solution(11447284156079240761)
XLA Ops:
  0.0 18.1 %prepare.1 = (bf16[96,288,128]{2,1,0:T(8,128)(2,1)S(1)}, f32[96,32,256]{2,1,0:T(8,128)S(1)}, f32[776,256]{1,0:T(8,128)S(1)}, s32[2,1,640]{2,1,0:T(1,128)S(1)}) custom-call(s32[4]{0:T(128)} %owner_hbm.1, f32[192,200]{1,0:T(8,128)} %bitcast.3, bf16[96,8192]{1,0:T(8,128)(2,1)} %x_ref.1, s32[1,96]{1,0:T(1,128)} %bitcast.5, s32[32,24]{1,0:T(8,128)} %bitcast.4), custom_call_target="tpu_custom_call" | custom-call | tf_op jit(solution)/shard_map/prepare/pallas_call | solution.py:380
  18.1 2.7 %pairs.3 = bf16[16,32,128]{2,1,0:T(8,128)(2,1)S(1)} custom-call(s32[2,1,640]{2,1,0:T(1,128)S(1)} %get-tuple-element.9.list_ref, bf16[96,288,128]{2,1,0:T(8,128)(2,1)S(1)} %get-tuple-element.10.z_ref, f32[96,32,256]{2,1,0:T(8,128)S(1)} %get-tuple-element.11.inv_ref, f32[776,256]{1,0:T(8,128)S(1)} %get-tuple-element.12.taps_ref), custom_call_target="tpu_custom_call" | custom-call | flops 402653184 | bytes 12582912 | tf_op jit(solution)/shard_map/pairs/pallas_call | solution.py:420
  20.8 1.5 %collective-permute-start = (bf16[16,32,128]{2,1,0:T(8,128)(2,1)S(1)}, bf16[16,32,128]{2,1,0:T(8,128)(2,1)S(1)}, u32[]{:S(2)}, u32[]{:S(2)}) collective-permute-start(bf16[16,32,128]{2,1,0:T(8,128)(2,1)S(1)} %pairs.3), channel_id=1, source_target_pairs={{0,1},{1,0},{2,3},{3,2},{4,5},{5,4},{6,7},{7,6},{8,9},{9,8},{10,11... | collective-permute-start | bytes 393224 | tf_op jit(solution)/shard_map/ppermute | solution.py:435
  22.4 2.7 %pairs.4 = bf16[16,32,128]{2,1,0:T(8,128)(2,1)S(1)} custom-call(s32[2,1,640]{2,1,0:T(1,128)S(1)} %get-tuple-element.9.list_ref, bf16[96,288,128]{2,1,0:T(8,128)(2,1)S(1)} %get-tuple-element.10.z_ref, f32[96,32,256]{2,1,0:T(8,128)S(1)} %get-tuple-element.11.inv_ref, f32[776,256]{1,0:T(8,128)S(1)} %get-tuple-element.12.taps_ref), custom_call_target="tpu_custom_call" | custom-call | flops 402653184 | bytes 12582912 | tf_op jit(solution)/shard_map/pairs/pallas_call | solution.py:420
  25.0 0.6 %collective-permute-start.1 = (bf16[16,32,128]{2,1,0:T(8,128)(2,1)S(1)}, bf16[16,32,128]{2,1,0:T(8,128)(2,1)S(1)}, u32[]{:S(2)}, u32[]{:S(2)}) collective-permute-start(bf16[16,32,128]{2,1,0:T(8,128)(2,1)S(1)} %pairs.4), channel_id=1, source_target_pairs={{0,1},{1,0},{2,3},{3,2},{4,5},{5,4},{6,7},{7,6},{8,9},{9,8},{10,11... | collective-permute-start | bytes 393224 | tf_op jit(solution)/shard_map/ppermute | solution.py:435
  25.7 4.0 %pairs.5.refs_2_ = f32[16,32,256]{2,1,0:T(8,128)S(1)} custom-call(s32[2,1,640]{2,1,0:T(1,128)S(1)} %get-tuple-element.9.list_ref, bf16[96,288,128]{2,1,0:T(8,128)(2,1)S(1)} %get-tuple-element.10.z_ref, f32[96,32,256]{2,1,0:T(8,128)S(1)} %get-tuple-element.11.inv_ref, f32[776,256]{1,0:T(8,128)S(1)} %get-tuple-element.12.taps_ref), custom_call_target="tpu_custom_call" | custom-call | flops 805306368 | bytes 12582912 | tf_op jit(solution)/shard_map/pairs/pallas_call | solution.py:420
  29.7 0.0 collective-permute-done.refs_0_
  29.7 0.6 %collective-permute-done.1.refs_1_ = bf16[16,32,128]{2,1,0:T(8,128)(2,1)S(1)} collective-permute-done((bf16[16,32,128]{2,1,0:T(8,128)(2,1)S(1)}, bf16[16,32,128]{2,1,0:T(8,128)(2,1)S(1)}, u32[]{:S(2)}, u32[]{:S(2)}) %collective-permute-start.1) | collective-permute-done | bytes 131104 | tf_op jit(solution)/shard_map/ppermute | solution.py:435
  30.3 7.1 %finish.1 = f32[16,64,128]{2,1,0:T(8,128)S(1)} custom-call(bf16[16,32,128]{2,1,0:T(8,128)(2,1)S(1)} %collective-permute-done.refs_0_, bf16[16,32,128]{2,1,0:T(8,128)(2,1)S(1)} %collective-permute-done.1.refs_1_, f32[16,32,256]{2,1,0:T(8,128)S(1)} %pairs.5.refs_2_), custom_call_target="tpu_custom_call" | custom-call | tf_op jit(solution)/shard_map/finish/pallas_call | solution.py:438
  37.4 1.0 %reshape.15 = f32[4,4,8192]{2,1,0:T(4,128)} reshape(f32[16,64,128]{2,1,0:T(8,128)S(1)} %finish.1) | data formatting | bytes 1048576 | tf_op jit(solution)/shard_map/reshape | solution.py:453
Async XLA Ops:
  20.8 8.9 %collective-permute-start = (bf16[16,32,128]{2,1,0:T(8,128)(2,1)S(1)}, bf16[16,32,128]{2,1,0:T(8,128)(2,1)S(1)}, u32[]{:S(2)}, u32[]{:S(2)}) collective-permute-start(bf16[16,32,128]{2,1,0:T(8,128)(2,1)S(1)} %pairs.3), channel_id=1, source_target_pairs={{0,1},{1,0},{2,3},{3,2},{4,5},{5,4},{6,7},{7,6},{8,9},{9,8},{10,11... | collective-permute-start | bytes 393224 | tf_op jit(solution)/shard_map/ppermute | solution.py:435
  25.0 5.3 %collective-permute-start.1 = (bf16[16,32,128]{2,1,0:T(8,128)(2,1)S(1)}, bf16[16,32,128]{2,1,0:T(8,128)(2,1)S(1)}, u32[]{:S(2)}, u32[]{:S(2)}) collective-permute-start(bf16[16,32,128]{2,1,0:T(8,128)(2,1)S(1)} %pairs.4), channel_id=1, source_target_pairs={{0,1},{1,0},{2,3},{3,2},{4,5},{5,4},{6,7},{7,6},{8,9},{9,8},{10,11... | collective-permute-start | bytes 393224 | tf_op jit(solution)/shard_map/ppermute | solution.py:435

commit v7 on v6

--- a/solution.py
+++ b/solution.py
@@ -12,6 +12,7 @@
 depth = 256
 rows_z = 288
 unroll = 64
+few = 16
 MESH = pl.DeviceIdType.MESH
 
 
@@ -302,14 +303,24 @@
         scale = inv_ref[col, :, first * 128 : (first + tiles) * 128]
         return [(codes[i] >> 17, product[i * offs : (i + 1) * offs] * scale) for i in range(2)]
 
-    def group(i, carry):
-        done = [entry(i * unroll + u) for u in range(unroll)]
+    def entries(start, size):
+        done = [entry(start + u) for u in range(size)]
         for both in done:
             for template, value in both:
                 acc_ref[template] += value
+
+    def group(i, carry):
+        entries(i * unroll, unroll)
         return carry
 
-    lax.fori_loop(0, (total + unroll - 1) // unroll, group, 0)
+    def small_group(i, carry):
+        entries(groups * unroll + i * few, few)
+        return carry
+
+    groups = (total + unroll - few - 1) // unroll
+    lax.fori_loop(0, groups, group, 0)
+    rest = jnp.maximum(total - groups * unroll, 0)
+    lax.fori_loop(0, (rest + few - 1) // few, small_group, 0)
     out_ref[...] = acc_ref[:held].astype(out_ref.dtype)
 
 

time: 38.5 us -> 38.5 us (level)
  no operation moved by 1% of the time
where the time goes in v7:
time: 38.5 us; the launch traced here: 38.4 us
  Pallas kernels  34.5 us (90%)
  starting transfers between devices  2.15 us (6%)
  local copies, waits for them, and re-layouts  1.01 us (3%)
  waiting for transfers between devices  0.64 us (2%)
    pallas_call x1, Pallas kernels, body(): pl.pallas_call(functools.partial(prepare_kernel, steps, count, regions),...  18.1 us
    pallas_call x3, Pallas kernels, partial_sums(): pl.pallas_call(functools.partial(pair_kernel, which, first), out_shape=ja...  9.35 us
    pallas_call x1, Pallas kernels, body(): pl.pallas_call(functools.partial(finish_kernel, time_local * count, count...  7.06 us
    ppermute x2, starting transfers between devices, body(): lax.ppermute(part, 'region', [(i, (i + d) % regions) for i in range(regio...  2.15 us
    reshape x1, local copies, waits for them, and re-layouts, body(): return result.reshape(steps, per, time_local)  1.01 us
  transfers between devices with their start and end apart: 2, of which 1 were waited for; matrix products, arithmetic and copies ran while one was open for 0% of the time, Pallas kernels for 17%

profile of v7, /device:TPU:0, one launch (start us, length us, event | category | flops | bytes accessed | tf_op | source)
XLA Modules:
  0.0 38.4 jit_solution(8880800148028810214)
XLA Ops:
  0.0 18.1 %prepare.1 = (bf16[96,288,128]{2,1,0:T(8,128)(2,1)S(1)}, f32[96,32,256]{2,1,0:T(8,128)S(1)}, f32[776,256]{1,0:T(8,128)S(1)}, s32[2,1,640]{2,1,0:T(1,128)S(1)}) custom-call(s32[4]{0:T(128)} %owner_hbm.1, f32[192,200]{1,0:T(8,128)} %bitcast.3, bf16[96,8192]{1,0:T(8,128)(2,1)} %x_ref.1, s32[1,96]{1,0:T(1,128)} %bitcast.5, s32[32,24]{1,0:T(8,128)} %bitcast.4), custom_call_target="tpu_custom_call" | custom-call | tf_op jit(solution)/shard_map/prepare/pallas_call | solution.py:391
  18.1 2.7 %pairs.3 = bf16[16,32,128]{2,1,0:T(8,128)(2,1)S(1)} custom-call(s32[2,1,640]{2,1,0:T(1,128)S(1)} %get-tuple-element.9.list_ref, bf16[96,288,128]{2,1,0:T(8,128)(2,1)S(1)} %get-tuple-element.10.z_ref, f32[96,32,256]{2,1,0:T(8,128)S(1)} %get-tuple-element.11.inv_ref, f32[776,256]{1,0:T(8,128)S(1)} %get-tuple-element.12.taps_ref), custom_call_target="tpu_custom_call" | custom-call | flops 402653184 | bytes 12582912 | tf_op jit(solution)/shard_map/pairs/pallas_call | solution.py:431
  20.8 1.6 %collective-permute-start = (bf16[16,32,128]{2,1,0:T(8,128)(2,1)S(1)}, bf16[16,32,128]{2,1,0:T(8,128)(2,1)S(1)}, u32[]{:S(2)}, u32[]{:S(2)}) collective-permute-start(bf16[16,32,128]{2,1,0:T(8,128)(2,1)S(1)} %pairs.3), channel_id=1, source_target_pairs={{0,1},{1,0},{2,3},{3,2},{4,5},{5,4},{6,7},{7,6},{8,9},{9,8},{10,11... | collective-permute-start | bytes 393224 | tf_op jit(solution)/shard_map/ppermute | solution.py:446
  22.3 2.7 %pairs.4 = bf16[16,32,128]{2,1,0:T(8,128)(2,1)S(1)} custom-call(s32[2,1,640]{2,1,0:T(1,128)S(1)} %get-tuple-element.9.list_ref, bf16[96,288,128]{2,1,0:T(8,128)(2,1)S(1)} %get-tuple-element.10.z_ref, f32[96,32,256]{2,1,0:T(8,128)S(1)} %get-tuple-element.11.inv_ref, f32[776,256]{1,0:T(8,128)S(1)} %get-tuple-element.12.taps_ref), custom_call_target="tpu_custom_call" | custom-call | flops 402653184 | bytes 12582912 | tf_op jit(solution)/shard_map/pairs/pallas_call | solution.py:431
  25.0 0.6 %collective-permute-start.1 = (bf16[16,32,128]{2,1,0:T(8,128)(2,1)S(1)}, bf16[16,32,128]{2,1,0:T(8,128)(2,1)S(1)}, u32[]{:S(2)}, u32[]{:S(2)}) collective-permute-start(bf16[16,32,128]{2,1,0:T(8,128)(2,1)S(1)} %pairs.4), channel_id=1, source_target_pairs={{0,1},{1,0},{2,3},{3,2},{4,5},{5,4},{6,7},{7,6},{8,9},{9,8},{10,11... | collective-permute-start | bytes 393224 | tf_op jit(solution)/shard_map/ppermute | solution.py:446
  25.6 4.0 %pairs.5.refs_2_ = f32[16,32,256]{2,1,0:T(8,128)S(1)} custom-call(s32[2,1,640]{2,1,0:T(1,128)S(1)} %get-tuple-element.9.list_ref, bf16[96,288,128]{2,1,0:T(8,128)(2,1)S(1)} %get-tuple-element.10.z_ref, f32[96,32,256]{2,1,0:T(8,128)S(1)} %get-tuple-element.11.inv_ref, f32[776,256]{1,0:T(8,128)S(1)} %get-tuple-element.12.taps_ref), custom_call_target="tpu_custom_call" | custom-call | flops 805306368 | bytes 12582912 | tf_op jit(solution)/shard_map/pairs/pallas_call | solution.py:431
  29.6 0.0 collective-permute-done.refs_0_
  29.7 0.6 %collective-permute-done.1.refs_1_ = bf16[16,32,128]{2,1,0:T(8,128)(2,1)S(1)} collective-permute-done((bf16[16,32,128]{2,1,0:T(8,128)(2,1)S(1)}, bf16[16,32,128]{2,1,0:T(8,128)(2,1)S(1)}, u32[]{:S(2)}, u32[]{:S(2)}) %collective-permute-start.1) | collective-permute-done | bytes 131104 | tf_op jit(solution)/shard_map/ppermute | solution.py:446
  30.3 7.1 %finish.1 = f32[16,64,128]{2,1,0:T(8,128)S(1)} custom-call(bf16[16,32,128]{2,1,0:T(8,128)(2,1)S(1)} %collective-permute-done.refs_0_, bf16[16,32,128]{2,1,0:T(8,128)(2,1)S(1)} %collective-permute-done.1.refs_1_, f32[16,32,256]{2,1,0:T(8,128)S(1)} %pairs.5.refs_2_), custom_call_target="tpu_custom_call" | custom-call | tf_op jit(solution)/shard_map/finish/pallas_call | solution.py:449
  37.4 1.0 %reshape.15 = f32[4,4,8192]{2,1,0:T(4,128)} reshape(f32[16,64,128]{2,1,0:T(8,128)S(1)} %finish.1) | data formatting | bytes 1048576 | tf_op jit(solution)/shard_map/reshape | solution.py:464
Async XLA Ops:
  20.8 8.9 %collective-permute-start = (bf16[16,32,128]{2,1,0:T(8,128)(2,1)S(1)}, bf16[16,32,128]{2,1,0:T(8,128)(2,1)S(1)}, u32[]{:S(2)}, u32[]{:S(2)}) collective-permute-start(bf16[16,32,128]{2,1,0:T(8,128)(2,1)S(1)} %pairs.3), channel_id=1, source_target_pairs={{0,1},{1,0},{2,3},{3,2},{4,5},{5,4},{6,7},{7,6},{8,9},{9,8},{10,11... | collective-permute-start | bytes 393224 | tf_op jit(solution)/shard_map/ppermute | solution.py:446
  25.0 5.3 %collective-permute-start.1 = (bf16[16,32,128]{2,1,0:T(8,128)(2,1)S(1)}, bf16[16,32,128]{2,1,0:T(8,128)(2,1)S(1)}, u32[]{:S(2)}, u32[]{:S(2)}) collective-permute-start(bf16[16,32,128]{2,1,0:T(8,128)(2,1)S(1)} %pairs.4), channel_id=1, source_target_pairs={{0,1},{1,0},{2,3},{3,2},{4,5},{5,4},{6,7},{7,6},{8,9},{9,8},{10,11... | collective-permute-start | bytes 393224 | tf_op jit(solution)/shard_map/ppermute | solution.py:446
